TPU v7x, 256 devices: a whole 4x4x8 slice. The times are simulated.
256 devices in a mesh: dom: 256 (over z, y, x, core).
Axes of the slice: x: 4, y: 4, z: 8, core: 2. Of those that a mesh axis runs over, the one named last changes fastest.
Arguments:
- adj_disp: float32 [1024, 33, 512], P('dom'), may hold values from -6 to 6
- adj_vel: float32 [1024, 33, 512], P('dom'), may hold values from -6 to 6
- fwd_disp: float32 [2, 1024, 33, 512], P(None, 'dom'), may hold values from -6 to 6
- shear_mod: float32 [2048, 25, 512], P('dom'), may hold values from 0.5 to 2
- inv_radius: float32 [2048, 25], P('dom'), may hold values from 0.001953125 to 0.0078125
- inv_mass: float32 [1024, 33], P('dom'), may hold values from 0.5 to 2
- mode_counts: int32 [2048], P('dom'), may hold values from 16 to 256, as said below
- rec_elem: int32 [256], P('dom'), may hold values from 0 to 2047
- rec_force: float32 [256, 2, 512], P('dom'), may hold values from -6 to 6
Outputs:
- new_disp: float32 [1024, 33, 512], P('dom')
- new_vel: float32 [1024, 33, 512], P('dom')
- kernel: float32 [2048, 25, 512], P('dom')
Inputs may be any that keep to these rules, and one draw needn't show every extreme that they name: `mode_counts`: in each device's aligned block of 8 elements exactly 2 elements have more than 128 modes; in each block at least one element has 256 modes and at least one has exactly 128.
All inputs are finite; a program needn't handle non-finite values.
Results may differ from a plain program's by a relative error of at most 0.0003.
Values sent between devices are 32-bit elements; how exact they have to be, the bound alone decides.
A program may use at most 128 MiB of HBM per device.

v0:
```python
import jax
import jax.numpy as jnp
import numpy as np
from jax import lax
from jax.sharding import PartitionSpec as P

GSCALE = 0.25
DTIME = 0.25


def from_behind(value, axis, steps):
    count = lax.axis_size(axis)
    leading, last = (max(0, -steps), min(count, count - steps))
    return lax.ppermute(value, axis, [(source, source + steps) for source in range(leading, last)])


def gll_derivative():
    points = np.array([-1.0, -np.sqrt(3.0 / 7.0), 0.0, np.sqrt(3.0 / 7.0), 1.0])
    legendre = (35.0 * points**4 - 30.0 * points**2 + 3.0) / 8.0
    matrix = np.zeros((5, 5))
    for row_off in range(5):
        for col_off in range(5):
            if row_off != col_off:
                matrix[row_off, col_off] = legendre[row_off] / (
                    legendre[col_off] * (points[row_off] - points[col_off])
                )
    matrix[0, 0] = -5.0
    matrix[4, 4] = 5.0
    return jnp.asarray(matrix, dtype=jnp.float32)


def dft_table(mode_width, samples):
    mode_index = jnp.arange(mode_width, dtype=jnp.int32)[:, None]
    sample_index = jnp.arange(samples, dtype=jnp.int32)[None, :]
    reduced = mode_index * sample_index % samples
    angles = 2.0 * np.pi / samples * reduced.astype(jnp.float32)
    factor = 1.0 / np.sqrt(mode_width)
    return jnp.concatenate([jnp.cos(angles) * factor, -jnp.sin(angles) * factor], axis=0)


def gather_elements(extended, elem_rows, elem_cols):
    pieces = []
    for row_off in range(5):
        for col_off in range(5):
            pieces.append(
                extended[
                    row_off : row_off + 4 * elem_rows : 4, col_off : col_off + 4 * elem_cols : 4
                ]
            )
    stacked = jnp.stack(pieces, axis=2)
    return stacked.reshape(elem_rows * elem_cols, 25, extended.shape[2])


def scatter_elements(contrib, elem_rows, elem_cols, node_cols):
    channels = contrib.shape[2]
    shaped = contrib.reshape(elem_rows, elem_cols, 25, channels)
    result = jnp.zeros((4 * elem_rows + 1, node_cols, channels), jnp.float32)
    for row_off in range(5):
        for col_off in range(5):
            result = result.at[
                row_off : row_off + 4 * elem_rows : 4, col_off : col_off + 4 * elem_cols : 4
            ].add(shaped[:, :, 5 * row_off + col_off])
    return result


def element_terms(values, fvalues, shear, inv_rad, counts, transform, mode_width):
    count_el = values.shape[0]
    samples = transform.shape[1]
    mode_index = jnp.arange(mode_width, dtype=jnp.int32)
    live_modes = (mode_index[None, :] < counts[:, None]).astype(jnp.float32)
    mode_mask = jnp.concatenate([live_modes, live_modes], axis=1)[:, None, :]
    factor = mode_index.astype(jnp.float32)
    derivative = gll_derivative()
    highest = lax.Precision.HIGHEST

    def gradients(field):
        masked = field * mode_mask
        element_grid = masked.reshape(count_el, 5, 5, 2 * mode_width)
        radial_grad = GSCALE * jnp.einsum(
            "ik,nkjc->nijc", derivative, element_grid, precision=highest
        )
        lateral_grad = GSCALE * jnp.einsum(
            "jk,nikc->nijc", derivative, element_grid, precision=highest
        )
        azimuth_grad = (
            jnp.concatenate(
                [-factor * masked[..., mode_width:], factor * masked[..., :mode_width]], axis=-1
            )
            * inv_rad[..., None]
        )
        outputs = []
        for gradient in (radial_grad, lateral_grad, azimuth_grad):
            outputs.append(
                jnp.dot(
                    gradient.reshape(count_el * 25, 2 * mode_width), transform, precision=highest
                )
            )
        return outputs

    adjoint = gradients(values)
    forward = gradients(fvalues)
    flat_shear = shear.reshape(count_el * 25, samples)
    returned = []
    for physical in adjoint:
        returned.append(jnp.dot(flat_shear * physical, transform.T, precision=highest))
    radial_back = GSCALE * jnp.einsum(
        "ik,nijc->nkjc",
        derivative,
        returned[0].reshape(count_el, 5, 5, 2 * mode_width),
        precision=highest,
    )
    lateral_back = GSCALE * jnp.einsum(
        "jk,nijc->nikc",
        derivative,
        returned[1].reshape(count_el, 5, 5, 2 * mode_width),
        precision=highest,
    )
    azimuth_back = returned[2].reshape(count_el, 25, 2 * mode_width) * inv_rad[..., None]
    azimuth_back = jnp.concatenate(
        [factor * azimuth_back[..., mode_width:], -factor * azimuth_back[..., :mode_width]], axis=-1
    )
    contrib = (
        radial_back.reshape(count_el, 25, 2 * mode_width)
        + lateral_back.reshape(count_el, 25, 2 * mode_width)
        + azimuth_back
    ) * mode_mask
    sensitivity = forward[0] * adjoint[0] + forward[1] * adjoint[1] + forward[2] * adjoint[2]
    return (contrib, sensitivity.reshape(count_el, 25, samples))


def element_block(values, fvalues, shear_mod, inv_radius, mode_counts, transform, mode_width):
    return element_terms(values, fvalues, shear_mod, inv_radius, mode_counts, transform, mode_width)


def per_device(
    adj_disp, adj_vel, fwd_disp, shear_mod, inv_radius, inv_mass, mode_counts, rec_elem, rec_force
):
    node_rows, node_cols, channels = adj_disp.shape
    mode_width = channels // 2
    nelem = mode_counts.shape[0]
    elem_cols = (node_cols - 1) // 4
    elem_rows = nelem // elem_cols
    step_count = fwd_disp.shape[0]
    transform = dft_table(mode_width, shear_mod.shape[2])
    forces, receiver_elems = (
        lax.all_gather(rec_force, "dom", axis=0, tiled=True),
        lax.all_gather(rec_elem, "dom", axis=0, tiled=True),
    )
    first_elem = lax.axis_index("dom") * nelem
    local_elem = receiver_elems - first_elem
    owned = (local_elem >= 0) & (local_elem < nelem)
    clamped = jnp.clip(local_elem, 0, nelem - 1)
    center_row = clamped // elem_cols * 4 + 2
    center_col = clamped % elem_cols * 4 + 2
    weighted = forces * owned.astype(jnp.float32)[:, None, None]
    source_load = (
        jnp.zeros((step_count, node_rows, node_cols, channels), jnp.float32)
        .at[:, center_row, center_col]
        .add(jnp.transpose(weighted, (1, 0, 2)))
    )
    kernel = None
    for step in range(step_count):
        adj_next, fwd_next = from_behind((adj_disp[0:1], fwd_disp[step, 0:1]), "dom", -1)
        extended = jnp.concatenate([adj_disp, adj_next], axis=0)
        fextended = jnp.concatenate([fwd_disp[step], fwd_next], axis=0)
        values = gather_elements(extended, elem_rows, elem_cols)
        fvalues = gather_elements(fextended, elem_rows, elem_cols)
        contrib, sensitivity = element_block(
            values, fvalues, shear_mod, inv_radius, mode_counts, transform, mode_width
        )
        stiffness = scatter_elements(contrib, elem_rows, elem_cols, node_cols)
        incoming = from_behind(stiffness[node_rows:], "dom", 1)
        stiffness = stiffness[:node_rows].at[0:1].add(incoming)
        adj_vel = adj_vel + DTIME * inv_mass[:, :, None] * (source_load[step] - stiffness)
        adj_disp = adj_disp + DTIME * adj_vel
        kernel = sensitivity if kernel is None else kernel + sensitivity
    return (adj_disp, adj_vel, kernel)


def solution(mesh):
    in_specs = (
        P("dom", None, None),
        P("dom", None, None),
        P(None, "dom", None, None),
        P("dom", None, None),
        P("dom", None),
        P("dom", None),
        P("dom"),
        P("dom"),
        P("dom", None, None),
    )
    out_specs = (P("dom", None, None), P("dom", None, None), P("dom", None, None))
    return jax.shard_map(
        per_device, mesh=mesh, in_specs=in_specs, out_specs=out_specs, check_vma=False
    )
```

profile of v0, /device:TPU:32, one launch (start us, length us, event | category | flops | bytes accessed | tf_op | source)
XLA Modules:
  0.0 375.5 jit_solution(14058817344552126806)
XLA Ops:
  8.1 6.1 %collective-permute-start = (f32[1,33,512]{2,1,0:T(8,128)S(1)}, f32[1,33,512]{2,1,0:T(8,128)S(1)}, u32[]{:S(2)}, u32[]{:S(2)}) collective-permute-start(f32[1,33,512]{2,1,0:T(8,128)S(1)} %copy.486), channel_id=1, source_target_pairs={{1,0},{2,1},{3,2},{4,3},{5,4},{6,5},{7,6},{8,7},{9,8},{10,9},{11,1... | collective-permute-start | bytes 202760 | tf_op jit(solution)/shard_map/ppermute | solution.py:14
  14.2 1.2 fusion.138
  16.0 2.6 collective-permute-start.4
  19.2 2.2 collective-permute-start.5
  22.3 2.1 negate_multiply_fusion
  29.2 78.7 %all-reduce.25 = s32[256]{0:T(256)S(1)} all-reduce(s32[256]{0:T(256)S(1)} %dynamic-update-slice.6), channel_id=1, replica_groups=mesh['dom'=256] {'dom'}, use_global_device_ids=true, to_apply=%add.25 | all-reduce | flops 256 | bytes 2048
  111.3 1.3 copy.315
  116.5 1.3 broadcast_multiply_fusion.5
  132.9 0.9 fusion.23
  133.8 0.9 fusion.19
  136.9 1.9 fusion.136
  138.8 1.2 fusion.61
  140.0 0.9 reshape.309
  140.9 2.0 fusion.21
  144.3 1.9 fusion.135
  146.2 1.2 fusion.59
  147.4 0.9 reshape.311
  148.3 1.8 fusion.142
  150.7 0.9 copy-done.21
  152.6 1.4 fusion.31
  154.0 1.9 fusion.57
  155.9 1.1 reshape.313
  159.6 0.9 pad_maximum_fusion.3
  195.9 1.9 collective-permute-start.1
  231.9 1.7 broadcast_multiply_fusion
  233.7 12.8 %scatter_fusion = f32[2,4,33,512]{3,0,2,1:T(2,128)S(1)} fusion(f32[2,4,33,512]{3,0,2,1:T(2,128)S(1)} %broadcast_in_dim.6, s32[256]{0:T(256)S(1)} %bitcast.498, f32[256,2,512]{2,1,0:T(2,128)S(1)} %broadcast_multiply_fusion), kind=kCustom, calls=%fused_computation | custom fusion | flops 262144 | bytes 3147776 | tf_op jit(solution)/shard_map/scatter-add | solution.py:159
  248.1 1.3 multiply_add_fusion.1
  249.5 8.0 %collective-permute-start.2 = (f32[1,33,512]{2,1,0:T(8,128)S(1)}, f32[1,33,512]{2,1,0:T(8,128)S(1)}, u32[]{:S(2)}, u32[]{:S(2)}) collective-permute-start(f32[1,33,512]{2,1,0:T(8,128)S(1)} %slice.985), channel_id=1, source_target_pairs={{1,0},{2,1},{3,2},{4,3},{5,4},{6,5},{7,6},{8,7},{9,8},{10,9},{11,1... | collective-permute-start | bytes 202760 | tf_op jit(solution)/shard_map/ppermute | solution.py:14
  258.3 1.0 collective-permute-done.2
  260.9 1.1 broadcast_multiply_fusion.1
  262.0 0.9 fusion.17
  262.9 0.9 fusion.13
  263.9 1.8 fusion.7
  265.7 1.8 fusion.5
  267.4 1.8 fusion.11
  269.2 1.8 fusion.9
  271.0 1.1 bitcast_multiply_fusion
  273.5 1.9 fusion.134
  277.6 0.9 slice_multiply_fusion.7
  279.4 1.2 fusion.55
  280.6 0.9 reshape.316
  281.6 2.0 fusion.15
  283.6 2.2 fusion.53
  285.7 1.9 reshape.318
  287.6 1.8 fusion.143
  291.9 1.9 fusion.51
  293.9 1.1 reshape.320
  294.9 1.0 copy_multiply_fusion.4
  296.0 1.0 copy-done.25
  298.6 1.1 copy.375
  299.7 1.2 reshape.326
  300.9 1.6 convolution_multiply_fusion.2
  302.8 1.1 copy.378
  303.9 1.2 reshape.327
  305.5 1.1 copy.365
  306.6 1.2 reshape.322
  307.8 1.6 convolution_multiply_fusion.5
  310.9 1.0 copy.369
  316.6 1.2 scatter_fusion.26
  353.9 2.3 collective-permute-start.3
  359.3 0.9 fusion.1
  360.4 1.0 copy.383
  361.4 2.7 collective-permute-done.3
  365.1 1.3 multiply_add_fusion
  (623 shorter events, 166.0 us)
Async XLA Ops:
  7.2 224.7 %all-gather.2.cloned.1.call-start = ((), (), s32[]{:S(2)}) async-start(), calls=%async_computation | async-start | bytes 1052672 | tf_op jit(solution)/shard_map/all_gather | solution.py:146
  8.1 123.5 %collective-permute-start = (f32[1,33,512]{2,1,0:T(8,128)S(1)}, f32[1,33,512]{2,1,0:T(8,128)S(1)}, u32[]{:S(2)}, u32[]{:S(2)}) collective-permute-start(f32[1,33,512]{2,1,0:T(8,128)S(1)} %copy.486), channel_id=1, source_target_pairs={{1,0},{2,1},{3,2},{4,3},{5,4},{6,5},{7,6},{8,7},{9,8},{10,9},{11,1... | collective-permute-start | bytes 202760 | tf_op jit(solution)/shard_map/ppermute | solution.py:14
  14.2 7.2 %copy-start.12 = (f32[4,33,512]{2,0,1:T(4,128)S(1)}, f32[4,33,512]{2,0,1:T(4,128)}, u32[]{:S(2)}) copy-start(f32[4,33,512]{2,0,1:T(4,128)} %param.15) | copy-start | bytes 811012
  16.0 141.4 %collective-permute-start.4 = (f32[1,33,512]{2,1,0:T(8,128)}, f32[1,33,512]{2,1,0:T(8,128)}, u32[]{:S(2)}, u32[]{:S(2)}) collective-permute-start(f32[1,33,512]{2,1,0:T(8,128)} %bitcast.497), channel_id=1, source_target_pairs={{1,0},{2,1},{3,2},{4,3},{5,4},{6,5},{7,6},{8,7},{9,8},{10,9},{11,1... | collective-permute-start | bytes 202760 | tf_op jit(solution)/shard_map/ppermute | solution.py:14
  19.2 140.3 %collective-permute-start.5 = (f32[1,33,512]{2,1,0:T(8,128)}, f32[1,33,512]{2,1,0:T(8,128)}, u32[]{:S(2)}, u32[]{:S(2)}) collective-permute-start(f32[1,33,512]{2,1,0:T(8,128)} %bitcast.496), channel_id=1, source_target_pairs={{1,0},{2,1},{3,2},{4,3},{5,4},{6,5},{7,6},{8,7},{9,8},{10,9},{11,1... | collective-permute-start | bytes 202760 | tf_op jit(solution)/shard_map/ppermute | solution.py:14
  22.3 2.6 copy-start.124
  22.3 86.7 %copy-start.32 = (f32[2,4,33,512]{3,1,2,0:T(4,128)S(1)}, f32[2,4,33,512]{3,1,2,0:T(4,128)}, u32[]{:S(2)}) copy-start(f32[2,4,33,512]{3,1,2,0:T(4,128)} %param.17) | copy-start | bytes 1622020
  112.6 5.8 %copy-start.112 = (f32[1,8,512]{2,1,0:T(8,128)S(1)}, f32[1,8,512]{2,1,0:T(8,128)}, u32[]{:S(2)}) copy-start(f32[1,8,512]{2,1,0:T(8,128)} %slice.820) | copy-start | bytes 49156
  112.6 12.9 %copy-start.126 = (s32[256]{0:T(256)S(1)}, s32[256]{0:T(256)}, u32[]{:S(2)}) copy-start(s32[256]{0:T(256)} %get-tuple-element.130) | copy-start | bytes 3076
  112.7 18.9 %copy-start.41 = (f32[5,33,512]{2,1,0:T(8,128)S(1)}, f32[5,33,512]{2,1,0:T(8,128)}, u32[]{:S(2)}) copy-start(f32[5,33,512]{2,1,0:T(8,128)} %constant_dynamic-update-slice_fusion.1) | copy-start | bytes 1013764
  122.5 61.5 %copy-start.43 = (s32[8]{0:T(128)}, s32[8]{0:T(128)S(1)}, u32[]{:S(2)}) copy-start(s32[8]{0:T(128)S(1)} %get-tuple-element.160) | copy-start | bytes 100
  124.2 62.3 %copy-start.53 = (s32[8]{0:T(128)}, s32[8]{0:T(128)S(1)}, u32[]{:S(2)}) copy-start(s32[8]{0:T(128)S(1)} %get-tuple-element.174) | copy-start | bytes 100
  124.8 64.2 %copy-start.49 = (s32[8]{0:T(128)}, s32[8]{0:T(128)S(1)}, u32[]{:S(2)}) copy-start(s32[8]{0:T(128)S(1)} %get-tuple-element.176) | copy-start | bytes 100
  125.4 66.2 %copy-start.47 = (s32[8]{0:T(128)}, s32[8]{0:T(128)S(1)}, u32[]{:S(2)}) copy-start(s32[8]{0:T(128)S(1)} %get-tuple-element.178) | copy-start | bytes 100
  125.4 67.1 %copy-start.51 = (s32[8]{0:T(128)}, s32[8]{0:T(128)S(1)}, u32[]{:S(2)}) copy-start(s32[8]{0:T(128)S(1)} %get-tuple-element.179) | copy-start | bytes 100
  125.4 68.0 %copy-start.45 = (s32[8]{0:T(128)}, s32[8]{0:T(128)S(1)}, u32[]{:S(2)}) copy-start(s32[8]{0:T(128)S(1)} %get-tuple-element.180) | copy-start | bytes 100
  138.8 1.2 copy-start.4
  146.2 1.2 copy-start.2
  150.7 1.0 copy-start.21
  150.7 1.0 copy-start.118
  150.7 1.0 copy-start.121
  154.0 2.0 copy-start
  155.9 1.1 copy-start.91
  195.9 35.4 %collective-permute-start.1 = (f32[1,33,512]{2,1,0:T(8,128)S(1)}, f32[1,33,512]{2,1,0:T(8,128)S(1)}, u32[]{:S(2)}, u32[]{:S(2)}) collective-permute-start(f32[1,33,512]{2,1,0:T(8,128)S(1)} %slice.983), channel_id=1, source_target_pairs={{0,1},{1,2},{2,3},{3,4},{4,5},{5,6},{6,7},{7,8},{8,9},{9,10},{10,1... | collective-permute-start | bytes 202760 | tf_op jit(solution)/shard_map/ppermute | solution.py:14
  247.0 1.1 copy-start.30
  247.0 2.3 copy-start.10
  249.5 9.9 %collective-permute-start.2 = (f32[1,33,512]{2,1,0:T(8,128)S(1)}, f32[1,33,512]{2,1,0:T(8,128)S(1)}, u32[]{:S(2)}, u32[]{:S(2)}) collective-permute-start(f32[1,33,512]{2,1,0:T(8,128)S(1)} %slice.985), channel_id=1, source_target_pairs={{1,0},{2,1},{3,2},{4,3},{5,4},{6,5},{7,6},{8,7},{9,8},{10,9},{11,1... | collective-permute-start | bytes 202760 | tf_op jit(solution)/shard_map/ppermute | solution.py:14
  259.7 1.1 copy-start.14
  259.7 1.1 copy-start.15
  269.2 1.8 copy-start.16
  269.2 1.8 copy-start.18
  276.0 1.0 copy-start.22
  276.0 1.1 copy-start.23
  276.0 1.2 copy-start.24
  276.0 1.2 copy-start.122
  290.0 1.0 copy-start.37
  290.0 1.0 copy-start.114
  294.9 1.0 copy-start.120
  294.9 1.0 copy-start.123
  295.9 1.0 copy-start.25
  297.0 1.4 copy-start.9
  300.9 1.7 copy-start.8
  303.9 1.3 copy-start.7
  306.6 1.2 copy-start.5
  307.8 1.7 copy-start.6
  311.9 1.0 copy-start.40
  312.9 1.0 copy-start.39
  314.0 1.0 copy-start.38
  316.6 1.2 copy-start.110
  344.8 8.1 %copy-start.93 = (s32[8]{0:T(128)S(1)}, s32[8]{0:T(128)}, u32[]{:S(2)}) copy-start(s32[8]{0:T(128)} %fusion.127) | copy-start | bytes 100
  352.0 4.3 %copy-start.27 = (f32[200,512]{1,0:T(8,128)S(1)}, f32[200,512]{1,0:T(8,128)}, u32[]{:S(2)}) copy-start(f32[200,512]{1,0:T(8,128)} %convolution_multiply_fusion.2) | copy-start | bytes 1228804
  353.8 3.3 copy-start.3
  353.8 3.3 copy-start.26
  353.9 3.3 copy-start.28
  353.9 10.3 %collective-permute-start.3 = (f32[1,33,512]{2,1,0:T(8,128)S(1)}, f32[1,33,512]{2,1,0:T(8,128)}, u32[]{:S(2)}, u32[]{:S(2)}) collective-permute-start(f32[1,33,512]{2,1,0:T(8,128)S(1)} %slice.1017), channel_id=1, source_target_pairs={{0,1},{1,2},{2,3},{3,4},{4,5},{5,6},{6,7},{7,8},{8,9},{9,10},{10,1... | collective-permute-start | bytes 202760 | tf_op jit(solution)/shard_map/ppermute | solution.py:14
  357.2 1.0 copy-start.1
  357.2 1.0 copy-start.33
  357.2 1.1 copy-start.35
  357.2 1.1 copy-start.115
  358.3 1.0 copy-start.36
  360.3 4.7 %copy-start.117 = (f32[4,33]{1,0:T(4,128)S(1)}, f32[4,33]{1,0:T(4,128)}, u32[]{:S(2)}) copy-start(f32[4,33]{1,0:T(4,128)} %broadcast_multiply_fusion.5) | copy-start | bytes 1588
  360.4 4.7 %copy-start.11 = (f32[1,4,33,512]{3,1,2,0:T(4,128)S(1)}, f32[1,4,33,512]{3,1,2,0:T(4,128)}, u32[]{:S(2)}) copy-start(f32[1,4,33,512]{3,1,2,0:T(4,128)} %copy-done.10) | copy-start | bytes 811012
  360.4 4.7 %copy-start.29 = (f32[1,4,33,512]{3,1,2,0:T(4,128)S(1)}, f32[1,4,33,512]{3,1,2,0:T(4,128)}, u32[]{:S(2)}) copy-start(f32[1,4,33,512]{3,1,2,0:T(4,128)} %copy.498) | copy-start | bytes 811012
  360.4 4.7 %copy-start.31 = (f32[4,33,512]{2,0,1:T(4,128)S(1)}, f32[4,33,512]{2,0,1:T(4,128)}, u32[]{:S(2)}) copy-start(f32[4,33,512]{2,0,1:T(4,128)} %param.16) | copy-start | bytes 811012
  (72 other events, 52.9 us)
Sparse Core Ops, SparseCore 0:
  14.3 101.8 all-gather.1
where the time goes:
time: 382 us; the launch traced here: 375 us
  local copies, waits for them, and re-layouts  118 us (31%)
  other arithmetic  89.9 us (24%)
  blocking collectives  78.7 us (21%)
  matrix products  43.9 us (11%)
  starting transfers between devices  23.2 us (6%)
  between operations  17.9 us (5%)
    unnamed x1, blocking collectives  78.7 us
    unnamed x364, local copies, waits for them, and re-layouts  71.8 us
    scatter-add x50, other arithmetic, scatter_elements(): result = result.at[row_off:row_off + 4 * elem_rows:4, col_off:col_off + 4...  45.6 us
    ppermute x6, starting transfers between devices, from_behind(): lax.ppermute(value, axis, [(source, source + steps) for source in range(l...  23.1 us
    dot_general x12, matrix products, gradients(): jnp.dot(gradient.reshape(count_el * 25, 2 * mode_width), transform, preci...  15.8 us
    scatter-add x1, other arithmetic, per_device(): source_load = jnp.zeros((step_count, node_rows, node_cols, channels), jnp...  12.8 us
    slice x96, local copies, waits for them, and re-layouts, gather_elements(): extended[row_off:row_off + 4 * elem_rows:4, col_off:col_off + 4 * elem_co...  10.8 us
    dot_general x6, matrix products, element_terms(): jnp.dot(flat_shear * physical, transform.T, precision=highest)  9.61 us
  transfers between devices with their start and end apart: 7, of which 2 were waited for; matrix products, arithmetic and copies ran while one was open for 32% of the time, Pallas kernels for 0%

commit v1 on v0

v1 whole, which is shorter than its diff:
```python
import functools

import jax
import jax.numpy as jnp
import ml_dtypes
import numpy as np
from jax import lax
from jax.experimental import pallas as pl
from jax.experimental.pallas import tpu as pltpu
from jax.sharding import PartitionSpec as P

GSCALE = 0.25
DTIME = 0.25
NZ, NY, NX, NCORE = 8, 4, 4, 2
NDEV = NZ * NY * NX * NCORE
BLOCKS = NCORE * NY * NX
LANES = 128
CHUNKS = 4
MODES = 256
WIDTH = 512
MESH = pl.DeviceIdType.MESH
F32 = jnp.float32
BF16 = jnp.bfloat16


def gll_derivative():
    points = np.array([-1.0, -np.sqrt(3.0 / 7.0), 0.0, np.sqrt(3.0 / 7.0), 1.0])
    legendre = (35.0 * points**4 - 30.0 * points**2 + 3.0) / 8.0
    matrix = np.zeros((5, 5))
    for row in range(5):
        for col in range(5):
            if row != col:
                matrix[row, col] = legendre[row] / (legendre[col] * (points[row] - points[col]))
    matrix[0, 0] = -5.0
    matrix[4, 4] = 5.0
    return matrix


DQ = GSCALE * gll_derivative()
DQT = DQ.T


def tables():
    mode = np.arange(MODES)[:, None]
    angle = 2.0 * np.pi * (mode * np.arange(WIDTH)[None, :] % WIDTH) / WIDTH
    scale = 1.0 / np.sqrt(MODES)
    cos, sin = np.cos(angle) * scale, np.sin(angle) * scale
    plain = np.concatenate([cos, -sin], axis=0)
    deriv = np.concatenate([-mode * sin, -mode * cos], axis=0)

    def parts(table):
        high = table.astype(ml_dtypes.bfloat16)
        low = (table - high.astype(np.float64)).astype(ml_dtypes.bfloat16)
        return high, low

    ph, plo = parts(plain)
    dh, dlo = parts(deriv)
    return np.stack([ph, dh, plo, dlo, ph.T, dh.T, plo.T, dlo.T])


def apply5(mat, x):
    even = [x[0] + x[4], x[1] + x[3]]
    odd = [x[0] - x[4], x[1] - x[3]]

    def combine(terms):
        total = None
        for coef, value in terms:
            if abs(coef) > 1e-12:
                term = float(coef) * value
                total = term if total is None else total + term
        return total

    out = [None] * 5
    for i in range(2):
        s = combine([(0.5 * (mat[i, k] - mat[i, 4 - k]), odd[k]) for k in range(2)])
        d = combine([(0.5 * (mat[i, k] + mat[i, 4 - k]), even[k]) for k in range(2)] + [(mat[i, 2], x[2])])
        out[i] = s + d
        out[4 - i] = s - d
    out[2] = combine([(mat[2, k], odd[k]) for k in range(2)])
    return out


def split(value):
    high = value.astype(BF16)
    return high, (value - high.astype(F32)).astype(BF16)


def dot(a, b):
    return lax.dot_general(a, b, (((1,), (0,)), ((), ())), preferred_element_type=F32)


def body(
    adj, vel, fwd, shear, inv_rad, inv_mass, counts, rec_elem, rec_force, table,
    out_v, out_w, out_k,
    v, w, f, tab, shraw, sh, irv, irb, imv, imn, imb, cnt, rel, rfv,
    ua, ud, fa, fd, q, z, kern, cc, cprev, cnext, mask,
    zbuf, zid, g0, g1, ebuf,
    lsem, tsem, osem, hs, hr, zs, zr, zis, zir, g0s, g0r, g1s, g1r, es, er, cs, cr,
):
    me = lax.axis_index("dom")
    mz, my, mx, mc = me // 32, (me // 8) % 4, (me // 2) % 4, me % 2
    nxt = (me + 1) % NDEV
    prv = (me + NDEV - 1) % NDEV
    zpeer = [((mz + k) % NZ) * 32 + me % 32 for k in range(1, NZ)]
    xpeer = [me - mx * 2 + ((mx + k) % NX) * 2 for k in range(1, NX)]
    ypeer = [me - my * 8 + ((my + k) % NY) * 8 for k in range(1, NY)]
    core = me + 1 - 2 * mc

    def local(src, dst, k):
        copy = pltpu.make_async_copy(src, dst, lsem.at[k])
        copy.start()
        return copy

    c_rf = local(rec_force, rfv, 0)
    c_rel = local(rec_elem, rel, 1)
    c_cnt = local(counts, cnt, 2)
    c_adj = [local(adj.at[:, :, pl.ds(LANES * c, LANES)], v.at[c, pl.ds(0, 4)], 3 + c) for c in range(4)]
    c_tab = []
    for k in range(8):
        copy = pltpu.make_async_copy(table.at[k], tab.at[k], tsem.at[k])
        c_tab.append(copy)
    for k in range(4):
        c_tab[k].start()
    c_f0 = [local(fwd.at[0, :, :, pl.ds(LANES * c, LANES)], f.at[0, c, pl.ds(0, 4)], 7 + c) for c in range(4)]
    c_ir = local(inv_rad, irv, 11)
    c_im = local(inv_mass, imv, 12)
    c_sh = local(shear, shraw, 13)
    for k in range(4, 8):
        c_tab[k].start()
    c_vel = [local(vel.at[:, :, pl.ds(LANES * c, LANES)], w.at[c, pl.ds(0, 4)], 14 + c) for c in range(4)]
    c_f1 = [local(fwd.at[1, :, :, pl.ds(LANES * c, LANES)], f.at[1, c, pl.ds(0, 4)], 18 + c) for c in range(4)]

    barrier = pltpu.get_barrier_semaphore()
    peers = zpeer + xpeer + ypeer + [core, nxt, prv]
    for peer in peers:
        pl.semaphore_signal(barrier, inc=1, device_id=(peer,), device_id_type=MESH)

    lane = lax.broadcasted_iota(jnp.int32, (8, WIDTH), 1)
    sub = lax.broadcasted_iota(jnp.int32, (8, WIDTH), 0)
    lane1 = lax.broadcasted_iota(jnp.int32, (1, LANES), 1)
    c_rf.wait()
    for s in range(2):
        for c in range(4):
            zbuf[pl.ds(mz * 8 + s * 4 + c, 1), :] = rfv[0, s : s + 1, LANES * c : LANES * (c + 1)]
    c_rel.wait()
    own_id = jnp.full((1, LANES), rel[0], jnp.int32).astype(F32) + 1.0
    zid[mz] = jnp.where(lane1 // 16 == mz, own_id, 0.0)

    pl.semaphore_wait(barrier, len(peers))

    def remote(src, dst, ssem, rsem, dev):
        copy = pltpu.make_async_remote_copy(
            src_ref=src, dst_ref=dst, send_sem=ssem, recv_sem=rsem, device_id=(dev,), device_id_type=MESH
        )
        copy.start()
        return copy

    zrow = pl.multiple_of(mz * 8, 8)
    z_copies = []
    for k in range(NZ - 1):
        z_copies.append(remote(zbuf.at[pl.ds(zrow, 8)], zbuf.at[pl.ds(zrow, 8)], zs.at[k], zr.at[k], zpeer[k]))
        z_copies.append(remote(zid.at[mz], zid.at[mz], zis.at[k], zir.at[k], zpeer[k]))
    h_adj, h_f0, h_vel, h_f1 = [], [], [], []
    for c in range(4):
        ls = pl.ds(LANES * c, LANES)
        h_adj.append(remote(adj.at[0, :, ls], v.at[c, 4], hs.at[c], hr.at[c], prv))
    for c in range(4):
        ls = pl.ds(LANES * c, LANES)
        h_f0.append(remote(fwd.at[0, 0, :, ls], f.at[0, c, 4], hs.at[4 + c], hr.at[4 + c], prv))
    h_im = remote(inv_mass, imn, hs.at[16], hr.at[16], prv)
    for c in range(4):
        ls = pl.ds(LANES * c, LANES)
        h_vel.append(remote(vel.at[0, :, ls], w.at[c, 4], hs.at[8 + c], hr.at[8 + c], prv))
    for c in range(4):
        ls = pl.ds(LANES * c, LANES)
        h_f1.append(remote(fwd.at[1, 0, :, ls], f.at[1, c, 4], hs.at[12 + c], hr.at[12 + c], prv))

    c_cnt.wait()
    limit = jnp.zeros((8, WIDTH), jnp.int32)
    for e in range(8):
        limit = jnp.where(sub == e, cnt[e], limit)
    live = (lane % MODES < limit).astype(F32)
    mask[0] = live
    mask[1] = live * jnp.where(me == NDEV - 1, 0.0, 1.0)

    def rows(ref, i):
        m = mask[1 if i == 4 else 0]
        out = []
        for j in range(5):
            value = jnp.concatenate([ref[c, i, pl.ds(j, 8, stride=4), :] for c in range(4)], axis=1)
            out.append(value * m)
        return out

    def transform(pieces, dests, first):
        high, low = split(jnp.concatenate(pieces, axis=0))
        plain = dot(high, tab[0]) + dot(low, tab[0]) + dot(high, tab[2])
        deriv = dot(high, tab[1]) + dot(low, tab[1]) + dot(high, tab[3])
        at = 0
        for dst, dst_d, offs in dests:
            for i in offs:
                dst[5 * i : 5 * i + 5] = plain[at : at + 40].reshape(5, 8, WIDTH)
                dst_d[5 * i : 5 * i + 5] = deriv[at : at + 40].reshape(5, 8, WIDTH)
                at += 40

    def gather(ref, offs):
        out = []
        for i in offs:
            out += rows(ref, i)
        return out

    for copy in c_adj + c_f0 + c_tab[:4]:
        copy.wait()
    f0, f1 = f.at[0], f.at[1]
    inner = [0, 1, 2, 3]
    transform(gather(v, inner) + gather(f0, inner), [(ua, ud, inner), (fa, fd, inner)], True)

    for copy in z_copies:
        copy.wait()
    own = mc * 16 + my * 4 + mx
    for s, g in ((0, g0), (1, g1)):
        for c in range(4):
            g[own, c] = zbuf[pl.ds(s * 4 + c, 8, stride=8), :]
    ids = zid[0]
    for k in range(1, NZ):
        ids = ids + zid[k]
    ebuf[own] = ids
    x0 = [remote(g0.at[own], g0.at[own], g0s.at[k], g0r.at[k], xpeer[k]) for k in range(3)]
    xe = [remote(ebuf.at[own], ebuf.at[own], es.at[k], er.at[k], xpeer[k]) for k in range(3)]
    x1 = [remote(g1.at[own], g1.at[own], g1s.at[k], g1r.at[k], xpeer[k]) for k in range(3)]

    c_ir.wait()
    for n in range(25):
        irb[n] = jnp.broadcast_to(irv[:, n : n + 1], (8, LANES))
    c_sh.wait()
    for n in range(25):
        sh[n] = shraw[:, n, :]

    for copy in h_adj + h_f0:
        copy.wait()
    transform(gather(v, [4]) + gather(f0, [4]), [(ua, ud, [4]), (fa, fd, [4])], False)

    def contraction(first):
        def chunk(c, carry):
            ls = pl.ds(pl.multiple_of(c * LANES, LANES), LANES)
            for j in range(5):
                ns = [5 * k + j for k in range(5)]
                pa = apply5(DQ, [ua[n, :, ls] for n in ns])
                pf = apply5(DQ, [fa[n, :, ls] for n in ns])
                s = [sh[n, :, ls] * p for n, p in zip(ns, pa)]
                back = apply5(DQT, s)
                for k, n in enumerate(ns):
                    q[n, :, ls] = back[k]
                    term = pa[k] * pf[k]
                    kern[n, :, ls] = term if first else kern[n, :, ls] + term
            for i in range(5):
                ns = [5 * i + k for k in range(5)]
                pa = apply5(DQ, [ua[n, :, ls] for n in ns])
                pf = apply5(DQ, [fa[n, :, ls] for n in ns])
                shs = [sh[n, :, ls] for n in ns]
                back = apply5(DQT, [a * b for a, b in zip(shs, pa)])
                for k, n in enumerate(ns):
                    q[n, :, ls] += back[k]
                    ir = irb[n]
                    p3 = ir * ud[n, :, ls]
                    kern[n, :, ls] += pa[k] * pf[k] + p3 * (ir * fd[n, :, ls])
                    z[n, :, ls] = ir * shs[k] * p3
            return carry

        lax.fori_loop(0, CHUNKS, chunk, 0)

    contraction(True)

    quad = pl.ds(pl.multiple_of(mc * 16 + my * 4, 4), 4)
    for copy in x0 + xe:
        copy.wait()
    y0 = [remote(g0.at[quad], g0.at[quad], g0s.at[3 + k], g0r.at[3 + k], ypeer[k]) for k in range(3)]
    ye = [remote(ebuf.at[quad], ebuf.at[quad], es.at[3 + k], er.at[3 + k], ypeer[k]) for k in range(3)]
    for copy in x1:
        copy.wait()
    y1 = [remote(g1.at[quad], g1.at[quad], g1s.at[3 + k], g1r.at[3 + k], ypeer[k]) for k in range(3)]

    for copy in c_tab[4:]:
        copy.wait()

    def back_rows(step, offs):
        rows_q = [q[5 * i : 5 * i + 5].reshape(40, WIDTH) for i in offs]
        rows_z = [z[5 * i : 5 * i + 5].reshape(40, WIDTH) for i in offs]
        qh, ql = split(jnp.concatenate(rows_q, axis=0))
        zh, zl = split(jnp.concatenate(rows_z, axis=0))
        total = dot(qh, tab[4]) + dot(ql, tab[4]) + dot(qh, tab[6])
        total = total + (dot(zh, tab[5]) + dot(zl, tab[5]) + dot(zh, tab[7]))
        m = mask[0]
        for at, i in enumerate(offs):
            cc[step, 5 * i : 5 * i + 5] = total[40 * at : 40 * at + 40].reshape(5, 8, WIDTH) * m[None]

    def image(step, i):
        parts = [cc[step, 5 * i + j] for j in range(5)]
        if i == 0:
            keep = jnp.where(me == 0, 0.0, 1.0)
            parts = [a + keep * cprev[step, j] for j, a in enumerate(parts)]
        if i == 4:
            parts = [a + cnext[j] for j, a in enumerate(parts)]
        return parts

    def wide(value):
        return jnp.concatenate([value] * 4, axis=1)

    def update(step, i, source=None):
        parts = image(step, i)
        turned = pltpu.roll(parts[4], 1, 0)
        cols = [parts[0] + jnp.where(sub == 0, 0.0, turned), parts[1], parts[2], parts[3]]
        for j in range(4):
            gain = DTIME * wide(imb[5 * i + j])
            load = -cols[j] if (source is None or j != 2) else source - cols[j]
            step_w = gain * load
            for c in range(4):
                at = pl.ds(j, 8, stride=4)
                new_w = w[c, i, at, :] + step_w[:, LANES * c : LANES * (c + 1)]
                w[c, i, at, :] = new_w
                v[c, i, at, :] += DTIME * new_w
        last = turned[0:1]
        for c in range(4):
            gain = DTIME * imb[5 * i + 4][0:1]
            new_w = w[c, i, 32:33, :] - gain * last[:, LANES * c : LANES * (c + 1)]
            w[c, i, 32:33, :] = new_w
            v[c, i, 32:33, :] += DTIME * new_w

    def ends(step):
        return (
            remote(cc.at[step, pl.ds(20, 5)], cprev.at[step], cs.at[2 * step], cr.at[2 * step], nxt),
            remote(cc.at[step, pl.ds(0, 5)], cnext, cs.at[2 * step + 1], cr.at[2 * step + 1], prv)
            if step == 0
            else None,
        )

    back_rows(0, [4, 0])
    up0, down0 = ends(0)
    back_rows(0, [1, 2, 3])

    c_im.wait()
    h_im.wait()
    lane33 = lax.broadcasted_iota(jnp.int32, (8, 33), 1)
    sub33 = lax.broadcasted_iota(jnp.int32, (8, 33), 0)
    for i in range(5):
        row = imv[i : i + 1, :] if i < 4 else imn[0:1, :]
        spread = jnp.broadcast_to(row, (8, 33))
        for j in range(4):
            picked = jnp.where(lane33 == 4 * sub33 + j, spread, 0.0)
            imb[5 * i + j] = jnp.broadcast_to(jnp.sum(picked, axis=1, keepdims=True), (8, LANES))
        imb[5 * i + 4] = jnp.broadcast_to(spread[:, 32:33], (8, LANES))
    for copy in c_vel + c_f1 + h_vel + h_f1:
        copy.wait()
    for i in (1, 2, 3):
        update(0, i)
    everything = [0, 1, 2, 3, 4]
    transform(gather(f1, everything), [(fa, fd, everything)], False)

    half = pl.ds(pl.multiple_of(mc * 16, 16), 16)
    for copy in y0 + ye:
        copy.wait()
    k0 = remote(g0.at[half], g0.at[half], g0s.at[6], g0r.at[6], core)
    ke = remote(ebuf.at[half], ebuf.at[half], es.at[6], er.at[6], core)
    for copy in y1:
        copy.wait()
    k1 = remote(g1.at[half], g1.at[half], g1s.at[6], g1r.at[6], core)

    up0.wait()
    down0.wait()
    update(0, 0)
    update(0, 4)
    transform(gather(v, everything), [(ua, ud, everything)], False)

    k0.wait()
    ke.wait()
    r_lane = lax.broadcasted_iota(jnp.int32, (BLOCKS, 8, LANES), 2)
    r_sub = lax.broadcasted_iota(jnp.int32, (BLOCKS, 8, LANES), 1)
    target = (me * 8 + 1 + r_lane % 16).astype(F32)
    hit = (jnp.broadcast_to(ebuf[...], (BLOCKS, 8, LANES)) == target) & (r_lane // 16 == r_sub) & (r_lane % 16 < 8)
    onehot = jnp.where(hit, 1.0, 0.0).reshape(BLOCKS * 8, LANES).T.astype(BF16)

    def source_of(g):
        outs = []
        for c in range(4):
            high, low = split(g[:, c].reshape(BLOCKS * 8, LANES))
            total = dot(onehot, high) + dot(onehot, low)
            acc = total[0:8]
            for k in range(1, 8):
                acc = acc + total[16 * k : 16 * k + 8]
            outs.append(acc)
        return jnp.concatenate(outs, axis=1)

    kick = DTIME * wide(imb[12]) * source_of(g0)
    shift = DTIME * kick
    for c in range(4):
        at = pl.ds(2, 8, stride=4)
        w[c, 2, at, :] += kick[:, LANES * c : LANES * (c + 1)]
        v[c, 2, at, :] += shift[:, LANES * c : LANES * (c + 1)]
    high, low = split(shift * mask[0])
    ua[12] += dot(high, tab[0]) + dot(low, tab[0]) + dot(high, tab[2])
    ud[12] += dot(high, tab[1]) + dot(low, tab[1]) + dot(high, tab[3])

    contraction(False)
    back_rows(1, [4, 0])
    up1, _ = ends(1)
    for n in range(25):
        shraw[:, n, :] = kern[n]
    o_k = pltpu.make_async_copy(shraw, out_k, osem.at[0])
    o_k.start()
    back_rows(1, [1, 2, 3])
    k1.wait()
    update(1, 2, source_of(g1))
    update(1, 1)
    update(1, 3)
    up1.wait()
    update(1, 0)
    outs = [o_k]
    for c in range(4):
        ls = pl.ds(LANES * c, LANES)
        copy = pltpu.make_async_copy(v.at[c, pl.ds(0, 4)], out_v.at[:, :, ls], osem.at[1 + c])
        copy.start()
        outs.append(copy)
        copy = pltpu.make_async_copy(w.at[c, pl.ds(0, 4)], out_w.at[:, :, ls], osem.at[5 + c])
        copy.start()
        outs.append(copy)
    for copy in outs:
        copy.wait()


def per_device(adj, vel, fwd, shear, inv_rad, inv_mass, counts, rec_elem, rec_force):
    table = jnp.asarray(tables())
    node = (4, 5, 33, LANES)
    elem = (25, 8, WIDTH)
    dma = pltpu.SemaphoreType.DMA
    scratch = [
        pltpu.VMEM(node, F32),
        pltpu.VMEM(node, F32),
        pltpu.VMEM((2,) + node, F32),
        pltpu.VMEM((8, WIDTH, WIDTH), BF16),
        pltpu.VMEM((8, 25, WIDTH), F32),
        pltpu.VMEM(elem, F32),
        pltpu.VMEM((8, 25), F32),
        pltpu.VMEM((25, 8, LANES), F32),
        pltpu.VMEM((4, 33), F32),
        pltpu.VMEM((4, 33), F32),
        pltpu.VMEM((25, 8, LANES), F32),
        pltpu.SMEM((8,), jnp.int32),
        pltpu.SMEM((1,), jnp.int32),
        pltpu.VMEM((1, 2, WIDTH), F32),
        pltpu.VMEM(elem, F32),
        pltpu.VMEM(elem, F32),
        pltpu.VMEM(elem, F32),
        pltpu.VMEM(elem, F32),
        pltpu.VMEM(elem, F32),
        pltpu.VMEM(elem, F32),
        pltpu.VMEM(elem, F32),
        pltpu.VMEM((2,) + elem, F32),
        pltpu.VMEM((2, 5, 8, WIDTH), F32),
        pltpu.VMEM((5, 8, WIDTH), F32),
        pltpu.VMEM((2, 8, WIDTH), F32),
        pltpu.VMEM((64, LANES), F32),
        pltpu.VMEM((NZ, 1, LANES), F32),
        pltpu.VMEM((BLOCKS, 4, 8, LANES), F32),
        pltpu.VMEM((BLOCKS, 4, 8, LANES), F32),
        pltpu.VMEM((BLOCKS, 1, LANES), F32),
        dma((22,)),
        dma((8,)),
        dma((9,)),
        dma((17,)),
        dma((17,)),
        dma((7,)),
        dma((7,)),
        dma((7,)),
        dma((7,)),
        dma((7,)),
        dma((7,)),
        dma((7,)),
        dma((7,)),
        dma((7,)),
        dma((7,)),
        dma((4,)),
        dma((4,)),
    ]
    shapes = [
        jax.ShapeDtypeStruct((4, 33, WIDTH), F32),
        jax.ShapeDtypeStruct((4, 33, WIDTH), F32),
        jax.ShapeDtypeStruct((8, 25, WIDTH), F32),
    ]
    return pl.pallas_call(
        body,
        out_shape=shapes,
        in_specs=[pl.BlockSpec(memory_space=pl.ANY)] * 10,
        out_specs=[pl.BlockSpec(memory_space=pl.ANY)] * 3,
        scratch_shapes=scratch,
        compiler_params=pltpu.CompilerParams(
            collective_id=0, has_side_effects=True, vmem_limit_bytes=48 * 2**20
        ),
        name="adjoint_steps",
    )(adj, vel, fwd, shear, inv_rad, inv_mass, counts, rec_elem, rec_force, table)


def solution(mesh):
    in_specs = (
        P("dom", None, None),
        P("dom", None, None),
        P(None, "dom", None, None),
        P("dom", None, None),
        P("dom", None),
        P("dom", None),
        P("dom"),
        P("dom"),
        P("dom", None, None),
    )
    out_specs = (P("dom", None, None), P("dom", None, None), P("dom", None, None))
    return jax.shard_map(per_device, mesh=mesh, in_specs=in_specs, out_specs=out_specs, check_vma=False)
```

time: 382 us -> 45.5 us (0.12)
  the two profiles are of different devices: /device:TPU:32 before, /device:TPU:0 now
where the time goes in v1:
time: 45.5 us; the launch traced here: 45.1 us
  Pallas kernels  33.8 us (74%)
  local copies, waits for them, and re-layouts  10 us (22%)
  between operations  1.32 us (3%)
    pallas_call x1, Pallas kernels, per_device(): pl.pallas_call(body, out_shape=shapes, in_specs=[pl.BlockSpec(memory_spac...  33.8 us
    unnamed x12, local copies, waits for them, and re-layouts  7.27 us
    pallas_call x3, local copies, waits for them, and re-layouts, per_device(): pl.pallas_call(body, out_shape=shapes, in_specs=[pl.BlockSpec(memory_spac...  2.75 us

profile of v1, /device:TPU:0, one launch (start us, length us, event | category | flops | bytes accessed | tf_op | source)
XLA Modules:
  0.0 45.1 jit_solution(11889015944514572190)
XLA Ops:
  1.3 1.0 %copy.13.adj = f32[4,33,512]{2,1,0:T(8,128)S(1)} copy(f32[4,33,512]{2,0,1:T(4,128)} %param.10) | data formatting | bytes 540672 | tf_op args[0]
  2.3 1.0 %copy.14.vel = f32[4,33,512]{2,1,0:T(8,128)S(1)} copy(f32[4,33,512]{2,0,1:T(4,128)} %param.11) | data formatting | bytes 540672 | tf_op args[1]
  3.4 1.2 %copy.16.shear = f32[8,25,512]{2,1,0:T(8,128)S(1)} copy(f32[8,25,512]{2,0,1:T(8,128)} %param.13) | data formatting | bytes 819200 | tf_op args[3]
  4.6 1.2 %copy.15.fwd = f32[2,4,33,512]{3,2,1,0:T(8,128)S(1)} copy(f32[2,4,33,512]{3,1,2,0:T(4,128)} %param.12) | data formatting | bytes 1081344 | tf_op args[2]
  5.9 0.0 copy-start
  5.9 0.7 %copy-done = f32[8,25]{1,0:T(8,128)S(1)} copy-done((f32[8,25]{1,0:T(8,128)S(1)}, f32[8,25]{1,0:T(8,128)}, u32[]{:S(2)}) %copy-start) | copy-done | bytes 824
  6.5 0.0 copy-start.1
  6.6 0.7 %copy-done.1 = f32[1,2,512]{2,1,0:T(2,128)S(1)} copy-done((f32[1,2,512]{2,1,0:T(2,128)S(1)}, f32[1,2,512]{2,1,0:T(2,128)}, u32[]{:S(2)}) %copy-start.1) | copy-done | bytes 4120
  7.2 0.0 copy-start.2
  7.2 0.7 %copy-done.2 = f32[4,33]{1,0:T(4,128)S(1)} copy-done((f32[4,33]{1,0:T(4,128)S(1)}, f32[4,33]{1,0:T(4,128)}, u32[]{:S(2)}) %copy-start.2) | copy-done | bytes 552
  7.9 0.0 copy-start.3
  7.9 0.7 %copy-done.3 = s32[8]{0:T(128)S(1)} copy-done((s32[8]{0:T(128)S(1)}, s32[8]{0:T(128)}, u32[]{:S(2)}) %copy-start.3) | copy-done | bytes 56
  8.6 33.8 %adjoint_steps.1 = (f32[4,33,512]{2,1,0:T(8,128)S(1)}, f32[4,33,512]{2,1,0:T(8,128)S(1)}, f32[8,25,512]{2,1,0:T(8,128)S(1)}) custom-call(f32[4,33,512]{2,1,0:T(8,128)S(1)} %copy.13.adj, f32[4,33,512]{2,1,0:T(8,128)S(1)} %copy.14.vel, f32[2,4,33,512]{3,2,1,0:T(8,128)S(1)} %copy.15.fwd, f32[8,25,512]{2,1,0:T(8,128)S(1)} %copy.16.shear, f32[8,25]{1,0:T(8,128)S(1)} %copy-done, ...), custom_call_target="tpu_custom_call" | custom-call | tf_op jit(solution)/shard_map/adjoint_steps/pallas_call | solution.py:488
  42.4 0.9 %copy.17 = f32[4,33,512]{2,0,1:T(4,128)} copy(f32[4,33,512]{2,1,0:T(8,128)S(1)} %get-tuple-element.3) | data formatting | bytes 540672 | tf_op jit(solution)/shard_map/adjoint_steps/pallas_call | solution.py:488
  43.2 0.9 %copy.18 = f32[4,33,512]{2,0,1:T(4,128)} copy(f32[4,33,512]{2,1,0:T(8,128)S(1)} %get-tuple-element.4) | data formatting | bytes 540672 | tf_op jit(solution)/shard_map/adjoint_steps/pallas_call | solution.py:488
  44.1 1.0 %copy.19 = f32[8,25,512]{2,0,1:T(8,128)} copy(f32[8,25,512]{2,1,0:T(8,128)S(1)} %get-tuple-element.5) | data formatting | bytes 819200 | tf_op jit(solution)/shard_map/adjoint_steps/pallas_call | solution.py:488
Async XLA Ops:
  5.9 0.7 %copy-start = (f32[8,25]{1,0:T(8,128)S(1)}, f32[8,25]{1,0:T(8,128)}, u32[]{:S(2)}) copy-start(f32[8,25]{1,0:T(8,128)} %inv_rad.1) | copy-start | bytes 2404
  6.5 0.7 %copy-start.1 = (f32[1,2,512]{2,1,0:T(2,128)S(1)}, f32[1,2,512]{2,1,0:T(2,128)}, u32[]{:S(2)}) copy-start(f32[1,2,512]{2,1,0:T(2,128)} %rec_force.1) | copy-start | bytes 12292
  7.2 0.7 %copy-start.2 = (f32[4,33]{1,0:T(4,128)S(1)}, f32[4,33]{1,0:T(4,128)}, u32[]{:S(2)}) copy-start(f32[4,33]{1,0:T(4,128)} %inv_mass.1) | copy-start | bytes 1588
  7.9 0.7 %copy-start.3 = (s32[8]{0:T(128)S(1)}, s32[8]{0:T(128)}, u32[]{:S(2)}) copy-start(s32[8]{0:T(128)} %counts.1) | copy-start | bytes 100

commit v2 on v1

v2 whole, which is shorter than its diff:
```python
import functools

import jax
import jax.numpy as jnp
import ml_dtypes
import numpy as np
from jax import lax
from jax.experimental import pallas as pl
from jax.experimental.pallas import tpu as pltpu
from jax.sharding import PartitionSpec as P

GSCALE = 0.25
DTIME = 0.25
NZ, NY, NX, NCORE = 8, 4, 4, 2
NDEV = NZ * NY * NX * NCORE
LANES = 128
CHUNKS = 4
MODES = 256
WIDTH = 512
MESH = pl.DeviceIdType.MESH
F32 = jnp.float32
BF16 = jnp.bfloat16


def gll_derivative():
    points = np.array([-1.0, -np.sqrt(3.0 / 7.0), 0.0, np.sqrt(3.0 / 7.0), 1.0])
    legendre = (35.0 * points**4 - 30.0 * points**2 + 3.0) / 8.0
    matrix = np.zeros((5, 5))
    for row in range(5):
        for col in range(5):
            if row != col:
                matrix[row, col] = legendre[row] / (legendre[col] * (points[row] - points[col]))
    matrix[0, 0] = -5.0
    matrix[4, 4] = 5.0
    return matrix


DQ = GSCALE * gll_derivative()
DQT = DQ.T


def tables():
    mode = np.arange(MODES)[:, None]
    angle = 2.0 * np.pi * (mode * np.arange(WIDTH)[None, :] % WIDTH) / WIDTH
    scale = 1.0 / np.sqrt(MODES)
    cos, sin = np.cos(angle) * scale, np.sin(angle) * scale
    plain = np.concatenate([cos, -sin], axis=0)
    deriv = np.concatenate([-mode * sin, -mode * cos], axis=0)

    def parts(table):
        high = table.astype(ml_dtypes.bfloat16)
        low = (table - high.astype(np.float64)).astype(ml_dtypes.bfloat16)
        return high, low

    ph, plo = parts(plain)
    dh, dlo = parts(deriv)
    return np.stack([ph, dh, plo, dlo, ph.T, dh.T, plo.T, dlo.T])


def apply5(mat, x):
    even = [x[0] + x[4], x[1] + x[3]]
    odd = [x[0] - x[4], x[1] - x[3]]

    def combine(terms):
        total = None
        for coef, value in terms:
            if abs(coef) > 1e-12:
                term = float(coef) * value
                total = term if total is None else total + term
        return total

    out = [None] * 5
    for i in range(2):
        s = combine([(0.5 * (mat[i, k] - mat[i, 4 - k]), odd[k]) for k in range(2)])
        d = combine([(0.5 * (mat[i, k] + mat[i, 4 - k]), even[k]) for k in range(2)] + [(mat[i, 2], x[2])])
        out[i] = s + d
        out[4 - i] = s - d
    out[2] = combine([(mat[2, k], odd[k]) for k in range(2)])
    return out


def split(value):
    high = value.astype(BF16)
    return high, (value - high.astype(F32)).astype(BF16)


def dot(a, b):
    return lax.dot_general(a, b, (((1,), (0,)), ((), ())), preferred_element_type=F32)


def body(
    adj, vel, fwd, shear, inv_rad, inv_mass, counts, rec_elem, rec_force, table,
    out_v, out_w, out_k,
    v, w, f, tab, sh, irv, irb, imv, imn, imb, cnt, rel,
    ua, ud, fa, fd, fa1, fd1, q, z, kern, cc, cprev, cnext, mask, halo, edge,
    cross, crossn, cb, zraw, zid, g0, g1, ebuf, psend, precv, pown,
    lsem, tsem, osem, hs, hr, zs, zr, zis, zir, g0s, g0r, g1s, g1r, es, er, cs, cr, ps, pr,
):
    me = lax.axis_index("dom")
    mz, my, mx, mc = me // 32, (me // 8) % 4, (me // 2) % 4, me % 2
    nxt = (me + 1) % NDEV
    prv = (me + NDEV - 1) % NDEV
    zpeer = [((mz + k) % NZ) * 32 + me % 32 for k in range(1, NZ)]
    shifts = [(0, 2), (2, 0), (2, 2), (1, 2), (2, 1), (3, 2), (2, 3), (1, 1), (1, 3), (3, 1), (3, 3), (0, 1), (1, 0), (0, 3), (3, 0)]
    ppeer = [mz * 32 + ((my + j) % NY) * 8 + ((mx + k) % NX) * 2 + mc for j, k in shifts]
    core = me + 1 - 2 * mc

    def local(src, dst, k):
        copy = pltpu.make_async_copy(src, dst, lsem.at[k])
        copy.start()
        return copy

    c_rf = local(rec_force.at[0], zraw.at[mz], 0)
    c_rel = local(rec_elem, rel, 1)
    c_cnt = local(counts, cnt, 2)
    c_adj = [local(adj.at[:, :, pl.ds(LANES * c, LANES)], v.at[c], 3 + c) for c in range(4)]
    c_tab = []
    for k in range(8):
        copy = pltpu.make_async_copy(table.at[k], tab.at[k], tsem.at[k])
        c_tab.append(copy)
    for k in range(4):
        c_tab[k].start()
    c_f0 = [local(fwd.at[0, :, :, pl.ds(LANES * c, LANES)], f.at[0, c], 7 + c) for c in range(4)]
    c_ir = local(inv_rad, irv, 11)
    c_im = local(inv_mass, imv, 12)
    c_sh = local(shear, sh, 13)
    for k in range(4, 8):
        c_tab[k].start()
    c_vel = [local(vel.at[:, :, pl.ds(LANES * c, LANES)], w.at[c], 14 + c) for c in range(4)]
    c_f1 = [local(fwd.at[1, :, :, pl.ds(LANES * c, LANES)], f.at[1, c], 18 + c) for c in range(4)]

    vv = [v.at[c].reshape(132, LANES) for c in range(4)]
    wv = [w.at[c].reshape(132, LANES) for c in range(4)]
    fv = [[f.at[s, c].reshape(132, LANES) for c in range(4)] for s in range(2)]

    def at(i, j):
        return pl.ds(4 * j + i, 8, stride=16)

    barrier = pltpu.get_barrier_semaphore()
    peers = zpeer + ppeer + [core]
    for peer in peers:
        pl.semaphore_signal(barrier, inc=1, device_id=(peer,), device_id_type=MESH)
    above, below = me < NDEV - 1, me > 0

    @pl.when(above)
    def _():
        pl.semaphore_signal(barrier, inc=1, device_id=(nxt,), device_id_type=MESH)

    @pl.when(below)
    def _():
        pl.semaphore_signal(barrier, inc=1, device_id=(prv,), device_id_type=MESH)

    lane = lax.broadcasted_iota(jnp.int32, (8, WIDTH), 1)
    sub = lax.broadcasted_iota(jnp.int32, (8, WIDTH), 0)
    lane1 = lax.broadcasted_iota(jnp.int32, (1, LANES), 1)
    missing = (me + NDEV - 1) // NDEV - me // (NDEV - 1)
    pl.semaphore_wait(barrier, len(peers) + 1 + missing)

    def remote(src, dst, ssem, rsem, dev):
        copy = pltpu.make_async_remote_copy(
            src_ref=src, dst_ref=dst, send_sem=ssem, recv_sem=rsem, device_id=(dev,), device_id_type=MESH
        )
        copy.start()
        return copy

    class Link:
        def __init__(self, src, dst, k, up, sems):
            self.sends, self.takes = (above, below) if up else (below, above)
            self.copy = pltpu.make_async_remote_copy(
                src_ref=src,
                dst_ref=dst,
                send_sem=sems[0].at[k],
                recv_sem=sems[1].at[k],
                device_id=(nxt if up else prv,),
                device_id_type=MESH,
            )

            @pl.when(self.sends)
            def _():
                self.copy.start()

        def wait(self):
            @pl.when(self.takes)
            def _():
                self.copy.wait_recv()

            @pl.when(self.sends)
            def _():
                self.copy.wait_send()

    z_copies = [remote(rec_force.at[0], zraw.at[mz], zs.at[k], zr.at[k], zpeer[k]) for k in range(NZ - 1)]
    c_rel.wait()
    own_id = jnp.full((1, LANES), rel[0], jnp.int32).astype(F32)
    zid[mz] = jnp.where(lane1 // 16 == mz, own_id, 0.0)
    id_copies = [remote(zid.at[mz], zid.at[mz], zis.at[k], zir.at[k], zpeer[k]) for k in range(NZ - 1)]

    def send_row(view, copies, k):
        for copy in copies:
            copy.wait()
        for j in range(5):
            for c in range(4):
                edge[k, j, :, LANES * c : LANES * (c + 1)] = view[c][at(0, j), :]
        return Link(edge.at[k], halo.at[k], k, False, (hs, hr))

    h_adj = send_row(vv, c_adj, 0)
    h_f0 = send_row(fv[0], c_f0, 1)
    h_im = Link(inv_mass, imn, 4, False, (hs, hr))

    c_cnt.wait()
    limit = jnp.zeros((8, WIDTH), jnp.int32)
    for e in range(8):
        limit = jnp.where(sub == e, cnt[e], limit)
    live = (lane % MODES < limit).astype(F32)
    mask[0] = live
    mask[1] = live * jnp.where(me == NDEV - 1, 0.0, 1.0)

    @pl.when(me == NDEV - 1)
    def _():
        halo[...] = jnp.zeros(halo.shape, F32)
        cnext[...] = jnp.zeros(cnext.shape, F32)
        imn[...] = jnp.zeros(imn.shape, F32)

    @pl.when(me == 0)
    def _():
        cprev[...] = jnp.zeros(cprev.shape, F32)
        crossn[...] = jnp.zeros(crossn.shape, F32)


    def rows(view, k, i):
        out = []
        for j in range(5):
            if i == 4:
                out.append(halo[k, j] * mask[1])
            else:
                out.append(jnp.concatenate([view[c][at(i, j), :] for c in range(4)], axis=1) * mask[0])
        return out

    def transform(pieces, dests):
        high, low = split(jnp.concatenate(pieces, axis=0))
        plain = dot(high, tab[0]) + dot(low, tab[0]) + dot(high, tab[2])
        deriv = dot(high, tab[1]) + dot(low, tab[1]) + dot(high, tab[3])
        at = 0
        for dst, dst_d, offs in dests:
            for i in offs:
                dst[5 * i : 5 * i + 5] = plain[at : at + 40].reshape(5, 8, WIDTH)
                dst_d[5 * i : 5 * i + 5] = deriv[at : at + 40].reshape(5, 8, WIDTH)
                at += 40

    def gather(view, k, offs):
        out = []
        for i in offs:
            out += rows(view, k, i)
        return out

    for copy in c_tab[:4]:
        copy.wait()
    inner = [0, 1, 2, 3]
    transform(gather(vv, 0, inner) + gather(fv[0], 1, inner), [(ua, ud, inner), (fa, fd, inner)])

    h_f1 = send_row(fv[1], c_f1, 3)
    h_vel = send_row(wv, c_vel, 2)
    transform(gather(fv[1], 3, inner), [(fa1, fd1, inner)])
    def wide(value):
        return jnp.concatenate([value] * 4, axis=1)

    c_ir.wait()
    for n in range(25):
        irb[n] = jnp.broadcast_to(irv[:, n : n + 1], (8, LANES))
    c_sh.wait()
    c_im.wait()
    lane33 = lax.broadcasted_iota(jnp.int32, (8, 33), 1)
    sub33 = lax.broadcasted_iota(jnp.int32, (8, 33), 0)
    def mass(i):
        row = imv[i : i + 1, :] if i < 4 else imn[0:1, :]
        spread = jnp.broadcast_to(row, (8, 33))
        for j in range(4 if i < 4 else 5):
            picked = jnp.where(lane33 == 4 * sub33 + j, spread, 0.0)
            imb[5 * i + j] = jnp.broadcast_to(jnp.sum(picked, axis=1, keepdims=True), (8, LANES))
        if i < 4:
            imb[5 * i + 4] = jnp.broadcast_to(spread[:, 32:33], (8, LANES))
    for i in range(4):
        mass(i)
    for k in range(5):
        cb[k] = sum(float(DQ[i, k] * DQ[i, 2]) * sh[5 * i + 2] for i in (0, 1, 3, 4))
        cb[5 + k] = sum(float(DQ[i, k] * DQ[i, 2]) * sh[10 + i] for i in (0, 1, 3, 4))
    cross[0] = (DTIME * DTIME) * wide(imb[12]) * mask[0]
    cross[1] = cb[4]
    cross[2] = mask[0]
    h_cross = Link(cross, crossn, 5, True, (hs, hr))

    h_adj.wait()
    h_f0.wait()
    transform(gather(vv, 0, [4]) + gather(fv[0], 1, [4]), [(ua, ud, [4]), (fa, fd, [4])])

    def contraction(first, fa, fd):
        def chunk(c, carry):
            ls = pl.ds(pl.multiple_of(c * LANES, LANES), LANES)
            for j in range(5):
                ns = [5 * k + j for k in range(5)]
                pa = apply5(DQ, [ua[n, :, ls] for n in ns])
                pf = apply5(DQ, [fa[n, :, ls] for n in ns])
                s = [sh[n, :, ls] * p for n, p in zip(ns, pa)]
                back = apply5(DQT, s)
                for k, n in enumerate(ns):
                    q[n, :, ls] = back[k]
                    term = pa[k] * pf[k]
                    kern[n, :, ls] = term if first else kern[n, :, ls] + term
            for i in range(5):
                ns = [5 * i + k for k in range(5)]
                pa = apply5(DQ, [ua[n, :, ls] for n in ns])
                pf = apply5(DQ, [fa[n, :, ls] for n in ns])
                shs = [sh[n, :, ls] for n in ns]
                back = apply5(DQT, [a * b for a, b in zip(shs, pa)])
                for k, n in enumerate(ns):
                    q[n, :, ls] += back[k]
                    ir = irb[n]
                    p3 = ir * ud[n, :, ls]
                    kern[n, :, ls] += pa[k] * pf[k] + p3 * (ir * fd[n, :, ls])
                    z[n, :, ls] = ir * shs[k] * p3
            return carry

        lax.fori_loop(0, CHUNKS, chunk, 0)

    contraction(True, fa, fd)

    for copy in c_tab[4:]:
        copy.wait()

    def back_rows(step, offs):
        rows_q = [q[5 * i : 5 * i + 5].reshape(40, WIDTH) for i in offs]
        rows_z = [z[5 * i : 5 * i + 5].reshape(40, WIDTH) for i in offs]
        qh, ql = split(jnp.concatenate(rows_q, axis=0))
        zh, zl = split(jnp.concatenate(rows_z, axis=0))
        total = dot(qh, tab[4]) + dot(ql, tab[4]) + dot(qh, tab[6])
        total = total + (dot(zh, tab[5]) + dot(zl, tab[5]) + dot(zh, tab[7]))
        m = mask[0]
        for at, i in enumerate(offs):
            cc[step, 5 * i : 5 * i + 5] = total[40 * at : 40 * at + 40].reshape(5, 8, WIDTH) * m[None]

    def image(step, i):
        parts = [cc[step, 5 * i + j] for j in range(5)]
        if i == 0:
            parts = [a + cprev[step, j] for j, a in enumerate(parts)]
        return parts

    def update(step, i):
        parts = image(step, i)
        turned = pltpu.roll(parts[4], 1, 0)
        cols = [parts[0] + jnp.where(sub == 0, 0.0, turned), parts[1], parts[2], parts[3]]
        for j in range(4):
            gain = DTIME * wide(imb[5 * i + j])
            step_w = gain * cols[j]
            for c in range(4):
                new_w = wv[c][at(i, j), :] - step_w[:, LANES * c : LANES * (c + 1)]
                wv[c][at(i, j), :] = new_w
                vv[c][at(i, j), :] += DTIME * new_w
        last = turned[0:1]
        for c in range(4):
            row = slice(128 + i, 129 + i)
            gain = DTIME * imb[5 * i + 4][0:1]
            new_w = wv[c][row, :] - gain * last[:, LANES * c : LANES * (c + 1)]
            wv[c][row, :] = new_w
            vv[c][row, :] += DTIME * new_w

    def update_halo():
        parts = [cc[0, 20 + j] + cnext[j] for j in range(5)]
        left = pltpu.roll(parts[4], 1, 0)
        right = pltpu.roll(parts[0], 7, 0)
        cols = [parts[0] + jnp.where(sub == 0, 0.0, left), parts[1], parts[2], parts[3]]
        cols.append(parts[4] + jnp.where(sub == 7, 0.0, right))
        for j in range(5):
            halo[0, j] += DTIME * (halo[2, j] - DTIME * wide(imb[20 + j]) * cols[j])

    def ends(step):
        up = Link(cc.at[step, pl.ds(20, 5)], cprev.at[step], 2 * step, True, (cs, cr))
        return up, Link(cc.at[step, pl.ds(0, 5)], cnext, 1, False, (cs, cr)) if step == 0 else None

    back_rows(0, [4, 0])
    up0, down0 = ends(0)
    own = my * 4 + mx
    c_rf.wait()
    for copy in z_copies:
        copy.wait()
    for c in range(4):
        g0[own, c] = zraw[:, 0, LANES * c : LANES * (c + 1)]
    p0 = [remote(g0.at[own], g0.at[own], g0s.at[k], g0r.at[k], ppeer[k]) for k in range(15)]
    for copy in id_copies:
        copy.wait()
    ids = zid[0]
    for k in range(1, NZ):
        ids = ids + zid[k]
    ebuf[own] = ids
    pe = [remote(ebuf.at[own], ebuf.at[own], es.at[k], er.at[k], ppeer[k]) for k in range(15)]
    for c in range(4):
        g1[own, c] = zraw[:, 1, LANES * c : LANES * (c + 1)]
    p1 = [remote(g1.at[own], g1.at[own], g1s.at[k], g1r.at[k], ppeer[k]) for k in range(15)]

    back_rows(0, [1, 2, 3])

    for i in (1, 2, 3):
        update(0, i)
    transform(gather(vv, 0, [1, 2, 3]), [(ua, ud, [1, 2, 3])])
    h_im.wait()
    mass(4)
    h_vel.wait()
    h_f1.wait()
    up0.wait()
    down0.wait()
    update(0, 0)
    update_halo()
    transform(gather(vv, 0, [0, 4]) + gather(fv[1], 3, [4]), [(ua, ud, [0, 4]), (fa1, fd1, [4])])

    contraction(False, fa1, fd1)
    back_rows(1, [4, 0])
    up1, _ = ends(1)
    outs = []

    def out_kernel(first, count, k):
        piece = pl.ds(first, count)
        copy = pltpu.make_async_copy(kern.at[piece], out_k.at[piece], osem.at[k])
        copy.start()
        outs.append(copy)

    for k, (first, count) in enumerate([(0, 2), (3, 4), (8, 2), (15, 2), (18, 4), (23, 2)]):
        out_kernel(first, count, k)
    back_rows(1, [1, 2, 3])
    for i in (1, 2, 3):
        update(1, i)
    for copy in p0 + pe:
        copy.wait()
    half = NY * NX
    r_lane = lax.broadcasted_iota(jnp.int32, (half, 8, LANES), 2)
    r_sub = lax.broadcasted_iota(jnp.int32, (half, 8, LANES), 1)
    group = r_lane // 16 == r_sub
    ids_all = jnp.broadcast_to(ebuf[...], (half, 8, LANES))

    def onehot(dev):
        target = ((dev - 1) * 8 + r_lane % 16).astype(F32)
        hit = (ids_all == target) & group
        return jnp.where(hit, 1.0, 0.0).reshape(half * 8, LANES).T.astype(BF16)

    pick = jnp.concatenate([onehot(core), onehot(me)], axis=0)

    def sums(g, k):
        for c in range(4):
            high, low = split(g[:, c].reshape(half * 8, LANES))
            total = dot(pick, high) + dot(pick, low)
            for d, ref in ((0, psend), (LANES, pown)):
                acc = total[d : d + 16]
                for t in range(1, 8):
                    acc = acc + total[d + 16 * t : d + 16 * t + 16]
                ref[k, :, LANES * c : LANES * (c + 1)] = acc
        return remote(psend.at[k], precv.at[k], ps.at[k], pr.at[k], core)

    k0 = sums(g0, 0)
    for copy in p1:
        copy.wait()
    k1 = sums(g1, 1)

    up1.wait()
    update(1, 0)
    h_cross.wait()

    k0.wait()
    source0 = pown[0] + precv[0]
    kick = DTIME * wide(imb[12]) * source0[8:16]
    high, low = split(jnp.concatenate([kick * (DTIME * mask[0]), crossn[0] * source0[0:8]], axis=0))
    plain = dot(high, tab[0]) + dot(low, tab[0]) + dot(high, tab[2])
    deriv = (dot(high, tab[1]) + dot(low, tab[1]) + dot(high, tab[3]))[0:8]
    before, plain = plain[8:16], plain[0:8]
    turn = wide(irb[12])
    col_f = apply5(DQ, [fa1[5 * k + 2] for k in range(5)])
    row_f = apply5(DQ, [fa1[10 + k] for k in range(5)])
    for k in (0, 1, 3, 4):
        kern[5 * k + 2] += float(DQ[k, 2]) * plain * col_f[k]
        kern[10 + k] += float(DQ[k, 2]) * plain * row_f[k]
    kern[12] += (turn * deriv) * (turn * fd1[12])
    for k, (first, count) in enumerate([(2, 1), (7, 1), (10, 5), (17, 1), (22, 1)]):
        out_kernel(first, count, 6 + k)
    terms = [cb[k] * plain for k in (0, 1, 3)] + [cb[5 + k] * plain for k in (0, 1, 3, 4)]
    terms += [crossn[1] * before, (cb[2] + cb[7]) * plain]
    high, low = split(jnp.concatenate(terms, axis=0))
    back = dot(high, tab[4]) + dot(low, tab[4]) + dot(high, tab[6])
    high, low = split(turn * turn * sh[12] * deriv)
    extra = dot(high, tab[5]) + dot(low, tab[5]) + dot(high, tab[7])
    b = [back[8 * k : 8 * k + 8] * mask[0] for k in range(7)]
    before = back[56:64] * crossn[2]
    middle = (back[64:72] + extra) * mask[0]
    turned = pltpu.roll(b[6], 1, 0)
    fix = {(0, 2): b[0] + before, (1, 2): b[1], (3, 2): b[2]}
    fix[(2, 0)] = b[3] + jnp.where(sub == 0, 0.0, turned)
    fix[(2, 1)], fix[(2, 3)], fix[(2, 2)] = b[4], b[5], middle
    k1.wait()
    kick1 = DTIME * wide(imb[12]) * (pown[1, 8:16] + precv[1, 8:16])
    for (i, j), value in fix.items():
        move = -(DTIME * wide(imb[5 * i + j])) * value
        shift = DTIME * move
        if (i, j) == (2, 2):
            move = move + kick + kick1
            shift = DTIME * (move + kick)
        for c in range(4):
            ls = slice(LANES * c, LANES * (c + 1))
            wv[c][at(i, j), :] += move[:, ls]
            vv[c][at(i, j), :] += shift[:, ls]
    for c in range(4):
        move = -(DTIME * imb[14][0:1]) * turned[0:1, LANES * c : LANES * (c + 1)]
        wv[c][130:131, :] += move
        vv[c][130:131, :] += DTIME * move
    for c in range(4):
        ls = pl.ds(LANES * c, LANES)
        copy = pltpu.make_async_copy(v.at[c], out_v.at[:, :, ls], osem.at[11 + c])
        copy.start()
        outs.append(copy)
        copy = pltpu.make_async_copy(w.at[c], out_w.at[:, :, ls], osem.at[15 + c])
        copy.start()
        outs.append(copy)
    for copy in outs:
        copy.wait()


def finish(a, b, c, oa, ob, oc, ta, tb, tc, sem):
    triples = [(a, ta, oa), (b, tb, ob), (c, tc, oc)]
    reads = [pltpu.make_async_copy(x, t, sem.at[k]) for k, (x, t, _) in enumerate(triples)]
    writes = [pltpu.make_async_copy(t, y, sem.at[3 + k]) for k, (_, t, y) in enumerate(triples)]
    for copy in reads:
        copy.start()
    for read, write in zip(reads, writes):
        read.wait()
        write.start()
    for copy in writes:
        copy.wait()


def per_device(adj, vel, fwd, shear, inv_rad, inv_mass, counts, rec_elem, rec_force):
    table = jnp.asarray(tables())
    node = (4, 33, 4, LANES)
    elem = (25, 8, WIDTH)
    dma = pltpu.SemaphoreType.DMA
    scratch = [
        pltpu.VMEM(node, F32),
        pltpu.VMEM(node, F32),
        pltpu.VMEM((2,) + node, F32),
        pltpu.VMEM((8, WIDTH, WIDTH), BF16),
        pltpu.VMEM(elem, F32),
        pltpu.VMEM((8, 25), F32),
        pltpu.VMEM((25, 8, LANES), F32),
        pltpu.VMEM((4, 33), F32),
        pltpu.VMEM((4, 33), F32),
        pltpu.VMEM((25, 8, LANES), F32),
        pltpu.SMEM((8,), jnp.int32),
        pltpu.SMEM((1,), jnp.int32),
        pltpu.VMEM(elem, F32),
        pltpu.VMEM(elem, F32),
        pltpu.VMEM(elem, F32),
        pltpu.VMEM(elem, F32),
        pltpu.VMEM(elem, F32),
        pltpu.VMEM(elem, F32),
        pltpu.VMEM(elem, F32),
        pltpu.VMEM(elem, F32),
        pltpu.VMEM(elem, F32),
        pltpu.VMEM((2,) + elem, F32),
        pltpu.VMEM((2, 5, 8, WIDTH), F32),
        pltpu.VMEM((5, 8, WIDTH), F32),
        pltpu.VMEM((2, 8, WIDTH), F32),
        pltpu.VMEM((4, 5, 8, WIDTH), F32),
        pltpu.VMEM((4, 5, 8, WIDTH), F32),
        pltpu.VMEM((3, 8, WIDTH), F32),
        pltpu.VMEM((3, 8, WIDTH), F32),
        pltpu.VMEM((10, 8, WIDTH), F32),
        pltpu.VMEM((NZ, 2, WIDTH), F32),
        pltpu.VMEM((NZ, 1, LANES), F32),
        pltpu.VMEM((NY * NX, 4, 8, LANES), F32),
        pltpu.VMEM((NY * NX, 4, 8, LANES), F32),
        pltpu.VMEM((NY * NX, 1, LANES), F32),
        pltpu.VMEM((2, 16, WIDTH), F32),
        pltpu.VMEM((2, 16, WIDTH), F32),
        pltpu.VMEM((2, 16, WIDTH), F32),
        dma((22,)),
        dma((8,)),
        dma((19,)),
        dma((6,)),
        dma((6,)),
        dma((7,)),
        dma((7,)),
        dma((7,)),
        dma((7,)),
        dma((15,)),
        dma((15,)),
        dma((15,)),
        dma((15,)),
        dma((15,)),
        dma((15,)),
        dma((4,)),
        dma((4,)),
        dma((2,)),
        dma((2,)),
    ]
    shapes = [
        jax.ShapeDtypeStruct((33, 4, WIDTH), F32),
        jax.ShapeDtypeStruct((33, 4, WIDTH), F32),
        jax.ShapeDtypeStruct((25, 8, WIDTH), F32),
    ]
    new_disp, new_vel, kernel = pl.pallas_call(
        body,
        out_shape=shapes,
        in_specs=[pl.BlockSpec(memory_space=pltpu.HBM)] * 10,
        out_specs=[pl.BlockSpec(memory_space=pltpu.HBM)] * 3,
        scratch_shapes=scratch,
        compiler_params=pltpu.CompilerParams(
            collective_id=0, has_side_effects=True, vmem_limit_bytes=63 * 2**20
        ),
        name="adjoint_steps",
    )(
        jnp.transpose(adj, (1, 0, 2)),
        jnp.transpose(vel, (1, 0, 2)),
        jnp.transpose(fwd, (0, 2, 1, 3)),
        jnp.transpose(shear, (1, 0, 2)),
        inv_rad,
        inv_mass,
        counts,
        rec_elem,
        rec_force,
        table,
    )
    outs = pl.pallas_call(
        finish,
        out_shape=shapes,
        in_specs=[pl.BlockSpec(memory_space=pltpu.HBM)] * 3,
        out_specs=[pl.BlockSpec(memory_space=pltpu.HBM)] * 3,
        scratch_shapes=[pltpu.VMEM(t.shape, F32) for t in shapes] + [dma((6,))],
        compiler_params=pltpu.CompilerParams(vmem_limit_bytes=63 * 2**20),
        name="results",
    )(new_disp, new_vel, kernel)
    return tuple(jnp.transpose(out, (1, 0, 2)) for out in outs)


def solution(mesh):
    in_specs = (
        P("dom", None, None),
        P("dom", None, None),
        P(None, "dom", None, None),
        P("dom", None, None),
        P("dom", None),
        P("dom", None),
        P("dom"),
        P("dom"),
        P("dom", None, None),
    )
    out_specs = (P("dom", None, None), P("dom", None, None), P("dom", None, None))
    return jax.shard_map(per_device, mesh=mesh, in_specs=in_specs, out_specs=out_specs, check_vma=False)
```

time: 45.5 us -> 33.7 us (0.74)
  the two profiles are of different devices: /device:TPU:0 before, /device:TPU:1 now
where the time goes in v2:
time: 33.7 us; the launch traced here: 33.6 us
  Pallas kernels  32.3 us (96%)
  between operations  1.29 us (4%)
    pallas_call x1, Pallas kernels, per_device(): pl.pallas_call(body, out_shape=shapes, in_specs=[pl.BlockSpec(memory_spac...  30.3 us
    pallas_call x1, Pallas kernels, per_device(): pl.pallas_call(finish, out_shape=shapes, in_specs=[pl.BlockSpec(memory_sp...  1.97 us

profile of v2, /device:TPU:1, one launch (start us, length us, event | category | flops | bytes accessed | tf_op | source)
XLA Modules:
  0.0 33.6 jit_solution(7983915863461854733)
XLA Ops:
  1.3 30.3 %adjoint_steps.1 = (f32[33,4,512]{2,1,0:T(4,128)}, f32[33,4,512]{2,1,0:T(4,128)}, f32[25,8,512]{2,1,0:T(8,128)}) custom-call(f32[33,4,512]{2,1,0:T(4,128)} %bitcast.9, f32[33,4,512]{2,1,0:T(4,128)} %bitcast.10, f32[2,33,4,512]{3,2,1,0:T(4,128)} %bitcast.7, f32[25,8,512]{2,1,0:T(8,128)} %bitcast.8, f32[8,25]{1,0:T(8,128)} %inv_rad.1, f32[4,33]{1,0:T(4,128)} %inv_mass.1, ...), custom_call_target="tpu_custom_call" | custom-call | tf_op jit(solution)/shard_map/adjoint_steps/pallas_call | solution.py:603
  31.6 2.0 %results.1 = (f32[33,4,512]{2,1,0:T(4,128)}, f32[33,4,512]{2,1,0:T(4,128)}, f32[25,8,512]{2,1,0:T(8,128)}) custom-call(f32[33,4,512]{2,1,0:T(4,128)} %get-tuple-element.9.a, f32[33,4,512]{2,1,0:T(4,128)} %get-tuple-element.10.b, f32[25,8,512]{2,1,0:T(8,128)} %get-tuple-element.11.c), custom_call_target="tpu_custom_call" | custom-call | tf_op jit(solution)/shard_map/results/pallas_call | solution.py:625

commit v3 on v2

--- a/solution.py
+++ b/solution.py
@@ -88,13 +88,24 @@
     return lax.dot_general(a, b, (((1,), (0,)), ((), ())), preferred_element_type=F32)
 
 
+def times(x, *parts):
+    rows = x.shape[0]
+    high = x.astype(BF16)
+    both = jnp.concatenate([x, x - high.astype(F32)], axis=0).astype(BF16)
+    out = []
+    for table_high, table_low in parts:
+        first = dot(both, table_high)
+        out.append(first[:rows] + first[rows:] + dot(high, table_low))
+    return out
+
+
 def body(
     adj, vel, fwd, shear, inv_rad, inv_mass, counts, rec_elem, rec_force, table,
     out_v, out_w, out_k,
     v, w, f, tab, sh, irv, irb, imv, imn, imb, cnt, rel,
     ua, ud, fa, fd, fa1, fd1, q, z, kern, cc, cprev, cnext, mask, halo, edge,
     cross, crossn, cb, zraw, zid, g0, g1, ebuf, psend, precv, pown,
-    lsem, tsem, osem, hs, hr, zs, zr, zis, zir, g0s, g0r, g1s, g1r, es, er, cs, cr, ps, pr,
+    lsem, tsem, osem, hs, hr, zs, zr, zis, zir, g0s, g0r, g1s, g1r, es, er, cs, cr, ps, pr, relay,
 ):
     me = lax.axis_index("dom")
     mz, my, mx, mc = me // 32, (me // 8) % 4, (me // 2) % 4, me % 2
@@ -103,7 +114,23 @@
     zpeer = [((mz + k) % NZ) * 32 + me % 32 for k in range(1, NZ)]
     shifts = [(0, 2), (2, 0), (2, 2), (1, 2), (2, 1), (3, 2), (2, 3), (1, 1), (1, 3), (3, 1), (3, 3), (0, 1), (1, 0), (0, 3), (3, 0)]
     ppeer = [mz * 32 + ((my + j) % NY) * 8 + ((mx + k) % NX) * 2 + mc for j, k in shifts]
+    xpeer = [me - mx * 2 + ((mx + k) % NX) * 2 for k in range(1, NX)]
+    ypeer = [me - my * 8 + ((my + k) % NY) * 8 for k in range(1, NY)]
     core = me + 1 - 2 * mc
+
+    barrier = pltpu.get_barrier_semaphore()
+    peers = zpeer + xpeer + ypeer + [core]
+    for peer in peers:
+        pl.semaphore_signal(barrier, inc=1, device_id=(peer,), device_id_type=MESH)
+    above, below = me < NDEV - 1, me > 0
+
+    @pl.when(above)
+    def _():
+        pl.semaphore_signal(barrier, inc=1, device_id=(nxt,), device_id_type=MESH)
+
+    @pl.when(below)
+    def _():
+        pl.semaphore_signal(barrier, inc=1, device_id=(prv,), device_id_type=MESH)
 
     def local(src, dst, k):
         copy = pltpu.make_async_copy(src, dst, lsem.at[k])
@@ -114,18 +141,15 @@
     c_rel = local(rec_elem, rel, 1)
     c_cnt = local(counts, cnt, 2)
     c_adj = [local(adj.at[:, :, pl.ds(LANES * c, LANES)], v.at[c], 3 + c) for c in range(4)]
-    c_tab = []
-    for k in range(8):
-        copy = pltpu.make_async_copy(table.at[k], tab.at[k], tsem.at[k])
-        c_tab.append(copy)
-    for k in range(4):
-        c_tab[k].start()
+    c_tab = [
+        pltpu.make_async_copy(table.at[pl.ds(4 * k, 4)], tab.at[pl.ds(4 * k, 4)], tsem.at[k]) for k in range(2)
+    ]
+    c_tab[0].start()
     c_f0 = [local(fwd.at[0, :, :, pl.ds(LANES * c, LANES)], f.at[0, c], 7 + c) for c in range(4)]
     c_ir = local(inv_rad, irv, 11)
     c_im = local(inv_mass, imv, 12)
     c_sh = local(shear, sh, 13)
-    for k in range(4, 8):
-        c_tab[k].start()
+    c_tab[1].start()
     c_vel = [local(vel.at[:, :, pl.ds(LANES * c, LANES)], w.at[c], 14 + c) for c in range(4)]
     c_f1 = [local(fwd.at[1, :, :, pl.ds(LANES * c, LANES)], f.at[1, c], 18 + c) for c in range(4)]
 
@@ -135,20 +159,6 @@
 
     def at(i, j):
         return pl.ds(4 * j + i, 8, stride=16)
-
-    barrier = pltpu.get_barrier_semaphore()
-    peers = zpeer + ppeer + [core]
-    for peer in peers:
-        pl.semaphore_signal(barrier, inc=1, device_id=(peer,), device_id_type=MESH)
-    above, below = me < NDEV - 1, me > 0
-
-    @pl.when(above)
-    def _():
-        pl.semaphore_signal(barrier, inc=1, device_id=(nxt,), device_id_type=MESH)
-
-    @pl.when(below)
-    def _():
-        pl.semaphore_signal(barrier, inc=1, device_id=(prv,), device_id_type=MESH)
 
     lane = lax.broadcasted_iota(jnp.int32, (8, WIDTH), 1)
     sub = lax.broadcasted_iota(jnp.int32, (8, WIDTH), 0)
@@ -206,6 +216,9 @@
     h_f0 = send_row(fv[0], c_f0, 1)
     h_im = Link(inv_mass, imn, 4, False, (hs, hr))
 
+    for peer in xpeer:
+        pl.semaphore_signal(relay, inc=1, device_id=(peer,), device_id_type=MESH)
+
     c_cnt.wait()
     limit = jnp.zeros((8, WIDTH), jnp.int32)
     for e in range(8):
@@ -236,9 +249,7 @@
         return out
 
     def transform(pieces, dests):
-        high, low = split(jnp.concatenate(pieces, axis=0))
-        plain = dot(high, tab[0]) + dot(low, tab[0]) + dot(high, tab[2])
-        deriv = dot(high, tab[1]) + dot(low, tab[1]) + dot(high, tab[3])
+        plain, deriv = times(jnp.concatenate(pieces, axis=0), (tab[0], tab[2]), (tab[1], tab[3]))
         at = 0
         for dst, dst_d, offs in dests:
             for i in offs:
@@ -252,8 +263,7 @@
             out += rows(view, k, i)
         return out
 
-    for copy in c_tab[:4]:
-        copy.wait()
+    c_tab[0].wait()
     inner = [0, 1, 2, 3]
     transform(gather(vv, 0, inner) + gather(fv[0], 1, inner), [(ua, ud, inner), (fa, fd, inner)])
 
@@ -292,10 +302,10 @@
     h_f0.wait()
     transform(gather(vv, 0, [4]) + gather(fv[0], 1, [4]), [(ua, ud, [4]), (fa, fd, [4])])
 
-    def contraction(first, fa, fd):
+    def contraction(first, fa, fd, offs):
         def chunk(c, carry):
             ls = pl.ds(pl.multiple_of(c * LANES, LANES), LANES)
-            for j in range(5):
+            for j in range(5) if 0 in offs else ():
                 ns = [5 * k + j for k in range(5)]
                 pa = apply5(DQ, [ua[n, :, ls] for n in ns])
                 pf = apply5(DQ, [fa[n, :, ls] for n in ns])
@@ -305,7 +315,7 @@
                     q[n, :, ls] = back[k]
                     term = pa[k] * pf[k]
                     kern[n, :, ls] = term if first else kern[n, :, ls] + term
-            for i in range(5):
+            for i in offs:
                 ns = [5 * i + k for k in range(5)]
                 pa = apply5(DQ, [ua[n, :, ls] for n in ns])
                 pf = apply5(DQ, [fa[n, :, ls] for n in ns])
@@ -321,18 +331,16 @@
 
         lax.fori_loop(0, CHUNKS, chunk, 0)
 
-    contraction(True, fa, fd)
-
-    for copy in c_tab[4:]:
-        copy.wait()
+    contraction(True, fa, fd, (0, 4))
+
+    c_tab[1].wait()
 
     def back_rows(step, offs):
         rows_q = [q[5 * i : 5 * i + 5].reshape(40, WIDTH) for i in offs]
         rows_z = [z[5 * i : 5 * i + 5].reshape(40, WIDTH) for i in offs]
-        qh, ql = split(jnp.concatenate(rows_q, axis=0))
-        zh, zl = split(jnp.concatenate(rows_z, axis=0))
-        total = dot(qh, tab[4]) + dot(ql, tab[4]) + dot(qh, tab[6])
-        total = total + (dot(zh, tab[5]) + dot(zl, tab[5]) + dot(zh, tab[7]))
+        (total,) = times(jnp.concatenate(rows_q, axis=0), (tab[4], tab[6]))
+        (azimuthal,) = times(jnp.concatenate(rows_z, axis=0), (tab[5], tab[7]))
+        total = total + azimuthal
         m = mask[0]
         for at, i in enumerate(offs):
             cc[step, 5 * i : 5 * i + 5] = total[40 * at : 40 * at + 40].reshape(5, 8, WIDTH) * m[None]
@@ -381,20 +389,22 @@
     c_rf.wait()
     for copy in z_copies:
         copy.wait()
-    for c in range(4):
-        g0[own, c] = zraw[:, 0, LANES * c : LANES * (c + 1)]
-    p0 = [remote(g0.at[own], g0.at[own], g0s.at[k], g0r.at[k], ppeer[k]) for k in range(15)]
     for copy in id_copies:
         copy.wait()
+    pl.semaphore_wait(relay, len(xpeer))
     ids = zid[0]
     for k in range(1, NZ):
         ids = ids + zid[k]
     ebuf[own] = ids
     pe = [remote(ebuf.at[own], ebuf.at[own], es.at[k], er.at[k], ppeer[k]) for k in range(15)]
     for c in range(4):
+        g0[own, c] = zraw[:, 0, LANES * c : LANES * (c + 1)]
+    p0 = [remote(g0.at[own], g0.at[own], g0s.at[k], g0r.at[k], ppeer[k]) for k in range(15)]
+    for c in range(4):
         g1[own, c] = zraw[:, 1, LANES * c : LANES * (c + 1)]
     p1 = [remote(g1.at[own], g1.at[own], g1s.at[k], g1r.at[k], ppeer[k]) for k in range(15)]
 
+    contraction(True, fa, fd, (1, 2, 3))
     back_rows(0, [1, 2, 3])
 
     for i in (1, 2, 3):
@@ -410,9 +420,10 @@
     update_halo()
     transform(gather(vv, 0, [0, 4]) + gather(fv[1], 3, [4]), [(ua, ud, [0, 4]), (fa1, fd1, [4])])
 
-    contraction(False, fa1, fd1)
+    contraction(False, fa1, fd1, (0, 4))
     back_rows(1, [4, 0])
     up1, _ = ends(1)
+    contraction(False, fa1, fd1, (1, 2, 3))
     outs = []
 
     def out_kernel(first, count, k):
@@ -426,7 +437,7 @@
     back_rows(1, [1, 2, 3])
     for i in (1, 2, 3):
         update(1, i)
-    for copy in p0 + pe:
+    for copy in pe:
         copy.wait()
     half = NY * NX
     r_lane = lax.broadcasted_iota(jnp.int32, (half, 8, LANES), 2)
@@ -440,6 +451,9 @@
         return jnp.where(hit, 1.0, 0.0).reshape(half * 8, LANES).T.astype(BF16)
 
     pick = jnp.concatenate([onehot(core), onehot(me)], axis=0)
+
+    for copy in p0:
+        copy.wait()
 
     def sums(g, k):
         for c in range(4):
@@ -456,21 +470,19 @@
     for copy in p1:
         copy.wait()
     k1 = sums(g1, 1)
-
     up1.wait()
     update(1, 0)
     h_cross.wait()
 
+    turn = wide(irb[12])
+    col_f = apply5(DQ, [fa1[5 * k + 2] for k in range(5)])
+    row_f = apply5(DQ, [fa1[10 + k] for k in range(5)])
     k0.wait()
     source0 = pown[0] + precv[0]
     kick = DTIME * wide(imb[12]) * source0[8:16]
-    high, low = split(jnp.concatenate([kick * (DTIME * mask[0]), crossn[0] * source0[0:8]], axis=0))
-    plain = dot(high, tab[0]) + dot(low, tab[0]) + dot(high, tab[2])
-    deriv = (dot(high, tab[1]) + dot(low, tab[1]) + dot(high, tab[3]))[0:8]
-    before, plain = plain[8:16], plain[0:8]
-    turn = wide(irb[12])
-    col_f = apply5(DQ, [fa1[5 * k + 2] for k in range(5)])
-    row_f = apply5(DQ, [fa1[10 + k] for k in range(5)])
+    moved = jnp.concatenate([kick * (DTIME * mask[0]), crossn[0] * source0[0:8]], axis=0)
+    plain, deriv = times(moved, (tab[0], tab[2]), (tab[1], tab[3]))
+    before, plain, deriv = plain[8:16], plain[0:8], deriv[0:8]
     for k in (0, 1, 3, 4):
         kern[5 * k + 2] += float(DQ[k, 2]) * plain * col_f[k]
         kern[10 + k] += float(DQ[k, 2]) * plain * row_f[k]
@@ -479,10 +491,8 @@
         out_kernel(first, count, 6 + k)
     terms = [cb[k] * plain for k in (0, 1, 3)] + [cb[5 + k] * plain for k in (0, 1, 3, 4)]
     terms += [crossn[1] * before, (cb[2] + cb[7]) * plain]
-    high, low = split(jnp.concatenate(terms, axis=0))
-    back = dot(high, tab[4]) + dot(low, tab[4]) + dot(high, tab[6])
-    high, low = split(turn * turn * sh[12] * deriv)
-    extra = dot(high, tab[5]) + dot(low, tab[5]) + dot(high, tab[7])
+    (back,) = times(jnp.concatenate(terms, axis=0), (tab[4], tab[6]))
+    (extra,) = times(turn * turn * sh[12] * deriv, (tab[5], tab[7]))
     b = [back[8 * k : 8 * k + 8] * mask[0] for k in range(7)]
     before = back[56:64] * crossn[2]
     middle = (back[64:72] + extra) * mask[0]
@@ -576,7 +586,7 @@
         pltpu.VMEM((2, 16, WIDTH), F32),
         pltpu.VMEM((2, 16, WIDTH), F32),
         dma((22,)),
-        dma((8,)),
+        dma((2,)),
         dma((19,)),
         dma((6,)),
         dma((6,)),
@@ -594,6 +604,7 @@
         dma((4,)),
         dma((2,)),
         dma((2,)),
+        pltpu.SemaphoreType.REGULAR,
     ]
     shapes = [
         jax.ShapeDtypeStruct((33, 4, WIDTH), F32),

time: 33.7 us -> 32.6 us (0.967)
  Pallas kernels: 32.3 us -> 31.2 us
    pallas_call x1, Pallas kernels: 30.3 us -> 29.2 us  [per_device(): pl.pallas_call(body, out_shape=shapes, in_specs=[pl.BlockSpec(memory_spac...]
where the time goes in v3:
time: 32.6 us; the launch traced here: 32.4 us
  Pallas kernels  31.2 us (96%)
  between operations  1.29 us (4%)
    pallas_call x1, Pallas kernels, per_device(): pl.pallas_call(body, out_shape=shapes, in_specs=[pl.BlockSpec(memory_spac...  29.2 us
    pallas_call x1, Pallas kernels, per_device(): pl.pallas_call(finish, out_shape=shapes, in_specs=[pl.BlockSpec(memory_sp...  1.97 us

profile of v3, /device:TPU:1, one launch (start us, length us, event | category | flops | bytes accessed | tf_op | source)
XLA Modules:
  0.0 32.4 jit_solution(15852373866031037674)
XLA Ops:
  1.3 29.2 %adjoint_steps.1 = (f32[33,4,512]{2,1,0:T(4,128)}, f32[33,4,512]{2,1,0:T(4,128)}, f32[25,8,512]{2,1,0:T(8,128)}) custom-call(f32[33,4,512]{2,1,0:T(4,128)} %bitcast.9, f32[33,4,512]{2,1,0:T(4,128)} %bitcast.10, f32[2,33,4,512]{3,2,1,0:T(4,128)} %bitcast.7, f32[25,8,512]{2,1,0:T(8,128)} %bitcast.8, f32[8,25]{1,0:T(8,128)} %inv_rad.1, f32[4,33]{1,0:T(4,128)} %inv_mass.1, ...), custom_call_target="tpu_custom_call" | custom-call | tf_op jit(solution)/shard_map/adjoint_steps/pallas_call | solution.py:614
  30.5 2.0 %results.1 = (f32[33,4,512]{2,1,0:T(4,128)}, f32[33,4,512]{2,1,0:T(4,128)}, f32[25,8,512]{2,1,0:T(8,128)}) custom-call(f32[33,4,512]{2,1,0:T(4,128)} %get-tuple-element.9.a, f32[33,4,512]{2,1,0:T(4,128)} %get-tuple-element.10.b, f32[25,8,512]{2,1,0:T(8,128)} %get-tuple-element.11.c), custom_call_target="tpu_custom_call" | custom-call | tf_op jit(solution)/shard_map/results/pallas_call | solution.py:636

commit v4 on v3

--- a/solution.py
+++ b/solution.py
@@ -101,9 +101,9 @@
 
 def body(
     adj, vel, fwd, shear, inv_rad, inv_mass, counts, rec_elem, rec_force, table,
-    out_v, out_w, out_k,
+    out_v, out_w, kern,
     v, w, f, tab, sh, irv, irb, imv, imn, imb, cnt, rel,
-    ua, ud, fa, fd, fa1, fd1, q, z, kern, cc, cprev, cnext, mask, halo, edge,
+    ua, ud, fa, fd, fa1, fd1, q, z, cc, cprev, cnext, mask, halo, edge,
     cross, crossn, cb, zraw, zid, g0, g1, ebuf, psend, precv, pown,
     lsem, tsem, osem, hs, hr, zs, zr, zis, zir, g0s, g0r, g1s, g1r, es, er, cs, cr, ps, pr, relay,
 ):
@@ -424,16 +424,6 @@
     back_rows(1, [4, 0])
     up1, _ = ends(1)
     contraction(False, fa1, fd1, (1, 2, 3))
-    outs = []
-
-    def out_kernel(first, count, k):
-        piece = pl.ds(first, count)
-        copy = pltpu.make_async_copy(kern.at[piece], out_k.at[piece], osem.at[k])
-        copy.start()
-        outs.append(copy)
-
-    for k, (first, count) in enumerate([(0, 2), (3, 4), (8, 2), (15, 2), (18, 4), (23, 2)]):
-        out_kernel(first, count, k)
     back_rows(1, [1, 2, 3])
     for i in (1, 2, 3):
         update(1, i)
@@ -470,8 +460,6 @@
     for copy in p1:
         copy.wait()
     k1 = sums(g1, 1)
-    up1.wait()
-    update(1, 0)
     h_cross.wait()
 
     turn = wide(irb[12])
@@ -487,8 +475,6 @@
         kern[5 * k + 2] += float(DQ[k, 2]) * plain * col_f[k]
         kern[10 + k] += float(DQ[k, 2]) * plain * row_f[k]
     kern[12] += (turn * deriv) * (turn * fd1[12])
-    for k, (first, count) in enumerate([(2, 1), (7, 1), (10, 5), (17, 1), (22, 1)]):
-        out_kernel(first, count, 6 + k)
     terms = [cb[k] * plain for k in (0, 1, 3)] + [cb[5 + k] * plain for k in (0, 1, 3, 4)]
     terms += [crossn[1] * before, (cb[2] + cb[7]) * plain]
     (back,) = times(jnp.concatenate(terms, axis=0), (tab[4], tab[6]))
@@ -502,6 +488,8 @@
     fix[(2, 1)], fix[(2, 3)], fix[(2, 2)] = b[4], b[5], middle
     k1.wait()
     kick1 = DTIME * wide(imb[12]) * (pown[1, 8:16] + precv[1, 8:16])
+    up1.wait()
+    update(1, 0)
     for (i, j), value in fix.items():
         move = -(DTIME * wide(imb[5 * i + j])) * value
         shift = DTIME * move
@@ -516,28 +504,24 @@
         move = -(DTIME * imb[14][0:1]) * turned[0:1, LANES * c : LANES * (c + 1)]
         wv[c][130:131, :] += move
         vv[c][130:131, :] += DTIME * move
+    outs = []
     for c in range(4):
         ls = pl.ds(LANES * c, LANES)
-        copy = pltpu.make_async_copy(v.at[c], out_v.at[:, :, ls], osem.at[11 + c])
+        copy = pltpu.make_async_copy(v.at[c], out_v.at[:, :, ls], osem.at[c])
         copy.start()
         outs.append(copy)
-        copy = pltpu.make_async_copy(w.at[c], out_w.at[:, :, ls], osem.at[15 + c])
+        copy = pltpu.make_async_copy(w.at[c], out_w.at[:, :, ls], osem.at[4 + c])
         copy.start()
         outs.append(copy)
     for copy in outs:
         copy.wait()
 
 
-def finish(a, b, c, oa, ob, oc, ta, tb, tc, sem):
-    triples = [(a, ta, oa), (b, tb, ob), (c, tc, oc)]
-    reads = [pltpu.make_async_copy(x, t, sem.at[k]) for k, (x, t, _) in enumerate(triples)]
-    writes = [pltpu.make_async_copy(t, y, sem.at[3 + k]) for k, (_, t, y) in enumerate(triples)]
-    for copy in reads:
+def finish(a, b, c, oa, ob, oc, sem):
+    copies = [pltpu.make_async_copy(x, y, sem.at[k]) for k, (x, y) in enumerate([(a, oa), (b, ob), (c, oc)])]
+    for copy in copies:
         copy.start()
-    for read, write in zip(reads, writes):
-        read.wait()
-        write.start()
-    for copy in writes:
+    for copy in copies:
         copy.wait()
 
 
@@ -559,7 +543,6 @@
         pltpu.VMEM((25, 8, LANES), F32),
         pltpu.SMEM((8,), jnp.int32),
         pltpu.SMEM((1,), jnp.int32),
-        pltpu.VMEM(elem, F32),
         pltpu.VMEM(elem, F32),
         pltpu.VMEM(elem, F32),
         pltpu.VMEM(elem, F32),
@@ -587,7 +570,7 @@
         pltpu.VMEM((2, 16, WIDTH), F32),
         dma((22,)),
         dma((2,)),
-        dma((19,)),
+        dma((8,)),
         dma((6,)),
         dma((6,)),
         dma((7,)),
@@ -613,12 +596,12 @@
     ]
     new_disp, new_vel, kernel = pl.pallas_call(
         body,
-        out_shape=shapes,
+        out_shape=[pltpu.VMEM(t.shape, F32) for t in shapes],
         in_specs=[pl.BlockSpec(memory_space=pltpu.HBM)] * 10,
-        out_specs=[pl.BlockSpec(memory_space=pltpu.HBM)] * 3,
+        out_specs=[pl.BlockSpec(memory_space=pltpu.VMEM)] * 3,
         scratch_shapes=scratch,
         compiler_params=pltpu.CompilerParams(
-            collective_id=0, has_side_effects=True, vmem_limit_bytes=63 * 2**20
+            collective_id=0, has_side_effects=True, vmem_limit_bytes=62 * 2**20
         ),
         name="adjoint_steps",
     )(
@@ -636,12 +619,11 @@
     outs = pl.pallas_call(
         finish,
         out_shape=shapes,
-        in_specs=[pl.BlockSpec(memory_space=pltpu.HBM)] * 3,
+        in_specs=[pl.BlockSpec(memory_space=pltpu.VMEM)] * 3,
         out_specs=[pl.BlockSpec(memory_space=pltpu.HBM)] * 3,
-        scratch_shapes=[pltpu.VMEM(t.shape, F32) for t in shapes] + [dma((6,))],
-        compiler_params=pltpu.CompilerParams(vmem_limit_bytes=63 * 2**20),
+        scratch_shapes=[dma((3,))],
         name="results",
-    )(new_disp, new_vel, kernel)
+    )(*(pltpu.with_memory_space_constraint(x, pltpu.VMEM) for x in (new_disp, new_vel, kernel)))
     return tuple(jnp.transpose(out, (1, 0, 2)) for out in outs)
 
 

time: 32.6 us -> 30.8 us (0.945)
  Pallas kernels: 31.2 us -> 29.4 us
    pallas_call x1, Pallas kernels: 1.97 us -> 0.96 us  [per_device(): pl.pallas_call(finish, out_shape=shapes, in_specs=[pl.BlockSpec(memory_sp...]
    pallas_call x1, Pallas kernels: 29.2 us -> 28.5 us  [per_device(): pl.pallas_call(body, out_shape=[pltpu.VMEM(t.shape, F32) for t in shapes]...]
where the time goes in v4:
time: 30.8 us; the launch traced here: 30.7 us
  Pallas kernels  29.4 us (95%)
  between operations  1.29 us (4%)
    pallas_call x1, Pallas kernels, per_device(): pl.pallas_call(body, out_shape=[pltpu.VMEM(t.shape, F32) for t in shapes]...  28.5 us
    pallas_call x1, Pallas kernels, per_device(): pl.pallas_call(finish, out_shape=shapes, in_specs=[pl.BlockSpec(memory_sp...  0.96 us

profile of v4, /device:TPU:1, one launch (start us, length us, event | category | flops | bytes accessed | tf_op | source)
XLA Modules:
  0.0 30.7 jit_solution(8737124212689118111)
XLA Ops:
  1.3 28.5 %adjoint_steps.1 = (f32[33,4,512]{2,1,0:T(4,128)S(1)}, f32[33,4,512]{2,1,0:T(4,128)S(1)}, f32[25,8,512]{2,1,0:T(8,128)S(1)}) custom-call(f32[33,4,512]{2,1,0:T(4,128)} %bitcast.9, f32[33,4,512]{2,1,0:T(4,128)} %bitcast.10, f32[2,33,4,512]{3,2,1,0:T(4,128)} %bitcast.7, f32[25,8,512]{2,1,0:T(8,128)} %bitcast.8, f32[8,25]{1,0:T(8,128)} %inv_rad.1, ...), custom_call_target="tpu_custom_call" | custom-call | tf_op jit(solution)/shard_map/adjoint_steps/pallas_call | solution.py:597
  29.7 1.0 %results.1 = (f32[33,4,512]{2,1,0:T(4,128)}, f32[33,4,512]{2,1,0:T(4,128)}, f32[25,8,512]{2,1,0:T(8,128)}) custom-call(f32[33,4,512]{2,1,0:T(4,128)S(1)} %get-tuple-element.9.a, f32[33,4,512]{2,1,0:T(4,128)S(1)} %get-tuple-element.10.b, f32[25,8,512]{2,1,0:T(8,128)S(1)} %get-tuple-element.11.c), custom_call_target="tpu_custom_call" | custom-call | tf_op jit(solution)/shard_map/results/pallas_call | solution.py:619

commit v5 on v4

--- a/solution.py
+++ b/solution.py
@@ -101,11 +101,11 @@
 
 def body(
     adj, vel, fwd, shear, inv_rad, inv_mass, counts, rec_elem, rec_force, table,
-    out_v, out_w, kern,
-    v, w, f, tab, sh, irv, irb, imv, imn, imb, cnt, rel,
+    v, w, kern,
+    f, tab, sh, irv, irb, imv, imn, imb, cnt, rel,
     ua, ud, fa, fd, fa1, fd1, q, z, cc, cprev, cnext, mask, halo, edge,
-    cross, crossn, cb, zraw, zid, g0, g1, ebuf, psend, precv, pown,
-    lsem, tsem, osem, hs, hr, zs, zr, zis, zir, g0s, g0r, g1s, g1r, es, er, cs, cr, ps, pr, relay,
+    cross, crossn, cb, zraw, zid, g0, psend, precv, pown,
+    lsem, tsem, hs, hr, zs, zr, zis, zir, g0s, g0r, cs, cr, ps, pr, relay,
 ):
     me = lax.axis_index("dom")
     mz, my, mx, mc = me // 32, (me // 8) % 4, (me // 2) % 4, me % 2
@@ -149,7 +149,6 @@
     c_ir = local(inv_rad, irv, 11)
     c_im = local(inv_mass, imv, 12)
     c_sh = local(shear, sh, 13)
-    c_tab[1].start()
     c_vel = [local(vel.at[:, :, pl.ds(LANES * c, LANES)], w.at[c], 14 + c) for c in range(4)]
     c_f1 = [local(fwd.at[1, :, :, pl.ds(LANES * c, LANES)], f.at[1, c], 18 + c) for c in range(4)]
 
@@ -162,7 +161,6 @@
 
     lane = lax.broadcasted_iota(jnp.int32, (8, WIDTH), 1)
     sub = lax.broadcasted_iota(jnp.int32, (8, WIDTH), 0)
-    lane1 = lax.broadcasted_iota(jnp.int32, (1, LANES), 1)
     missing = (me + NDEV - 1) // NDEV - me // (NDEV - 1)
     pl.semaphore_wait(barrier, len(peers) + 1 + missing)
 
@@ -201,7 +199,7 @@
     z_copies = [remote(rec_force.at[0], zraw.at[mz], zs.at[k], zr.at[k], zpeer[k]) for k in range(NZ - 1)]
     c_rel.wait()
     own_id = jnp.full((1, LANES), rel[0], jnp.int32).astype(F32)
-    zid[mz] = jnp.where(lane1 // 16 == mz, own_id, 0.0)
+    zid[mz] = own_id
     id_copies = [remote(zid.at[mz], zid.at[mz], zis.at[k], zir.at[k], zpeer[k]) for k in range(NZ - 1)]
 
     def send_row(view, copies, k):
@@ -267,6 +265,7 @@
     inner = [0, 1, 2, 3]
     transform(gather(vv, 0, inner) + gather(fv[0], 1, inner), [(ua, ud, inner), (fa, fd, inner)])
 
+    c_tab[1].start()
     h_f1 = send_row(fv[1], c_f1, 3)
     h_vel = send_row(wv, c_vel, 2)
     transform(gather(fv[1], 3, inner), [(fa1, fd1, inner)])
@@ -329,7 +328,7 @@
                     z[n, :, ls] = ir * shs[k] * p3
             return carry
 
-        lax.fori_loop(0, CHUNKS, chunk, 0)
+        lax.fori_loop(0, CHUNKS, chunk, 0, unroll=True)
 
     contraction(True, fa, fd, (0, 4))
 
@@ -392,17 +391,12 @@
     for copy in id_copies:
         copy.wait()
     pl.semaphore_wait(relay, len(xpeer))
-    ids = zid[0]
-    for k in range(1, NZ):
-        ids = ids + zid[k]
-    ebuf[own] = ids
-    pe = [remote(ebuf.at[own], ebuf.at[own], es.at[k], er.at[k], ppeer[k]) for k in range(15)]
+    for k in range(NZ):
+        g0[own, 4, k : k + 1, :] = zid[k]
     for c in range(4):
         g0[own, c] = zraw[:, 0, LANES * c : LANES * (c + 1)]
+        g0[own, 5 + c] = zraw[:, 1, LANES * c : LANES * (c + 1)]
     p0 = [remote(g0.at[own], g0.at[own], g0s.at[k], g0r.at[k], ppeer[k]) for k in range(15)]
-    for c in range(4):
-        g1[own, c] = zraw[:, 1, LANES * c : LANES * (c + 1)]
-    p1 = [remote(g1.at[own], g1.at[own], g1s.at[k], g1r.at[k], ppeer[k]) for k in range(15)]
 
     contraction(True, fa, fd, (1, 2, 3))
     back_rows(0, [1, 2, 3])
@@ -427,13 +421,13 @@
     back_rows(1, [1, 2, 3])
     for i in (1, 2, 3):
         update(1, i)
-    for copy in pe:
+    for copy in p0:
         copy.wait()
     half = NY * NX
     r_lane = lax.broadcasted_iota(jnp.int32, (half, 8, LANES), 2)
     r_sub = lax.broadcasted_iota(jnp.int32, (half, 8, LANES), 1)
     group = r_lane // 16 == r_sub
-    ids_all = jnp.broadcast_to(ebuf[...], (half, 8, LANES))
+    ids_all = g0[:, 4]
 
     def onehot(dev):
         target = ((dev - 1) * 8 + r_lane % 16).astype(F32)
@@ -442,12 +436,9 @@
 
     pick = jnp.concatenate([onehot(core), onehot(me)], axis=0)
 
-    for copy in p0:
-        copy.wait()
-
-    def sums(g, k):
+    def sums(first, k):
         for c in range(4):
-            high, low = split(g[:, c].reshape(half * 8, LANES))
+            high, low = split(g0[:, first + c].reshape(half * 8, LANES))
             total = dot(pick, high) + dot(pick, low)
             for d, ref in ((0, psend), (LANES, pown)):
                 acc = total[d : d + 16]
@@ -456,10 +447,8 @@
                 ref[k, :, LANES * c : LANES * (c + 1)] = acc
         return remote(psend.at[k], precv.at[k], ps.at[k], pr.at[k], core)
 
-    k0 = sums(g0, 0)
-    for copy in p1:
-        copy.wait()
-    k1 = sums(g1, 1)
+    k0 = sums(0, 0)
+    k1 = sums(5, 1)
     h_cross.wait()
 
     turn = wide(irb[12])
@@ -504,21 +493,14 @@
         move = -(DTIME * imb[14][0:1]) * turned[0:1, LANES * c : LANES * (c + 1)]
         wv[c][130:131, :] += move
         vv[c][130:131, :] += DTIME * move
-    outs = []
-    for c in range(4):
-        ls = pl.ds(LANES * c, LANES)
-        copy = pltpu.make_async_copy(v.at[c], out_v.at[:, :, ls], osem.at[c])
-        copy.start()
-        outs.append(copy)
-        copy = pltpu.make_async_copy(w.at[c], out_w.at[:, :, ls], osem.at[4 + c])
-        copy.start()
-        outs.append(copy)
-    for copy in outs:
-        copy.wait()
 
 
 def finish(a, b, c, oa, ob, oc, sem):
-    copies = [pltpu.make_async_copy(x, y, sem.at[k]) for k, (x, y) in enumerate([(a, oa), (b, ob), (c, oc)])]
+    copies = [pltpu.make_async_copy(c, oc, sem.at[8])]
+    for k in range(4):
+        ls = pl.ds(LANES * k, LANES)
+        copies.append(pltpu.make_async_copy(a.at[k], oa.at[:, :, ls], sem.at[k]))
+        copies.append(pltpu.make_async_copy(b.at[k], ob.at[:, :, ls], sem.at[4 + k]))
     for copy in copies:
         copy.start()
     for copy in copies:
@@ -531,8 +513,6 @@
     elem = (25, 8, WIDTH)
     dma = pltpu.SemaphoreType.DMA
     scratch = [
-        pltpu.VMEM(node, F32),
-        pltpu.VMEM(node, F32),
         pltpu.VMEM((2,) + node, F32),
         pltpu.VMEM((8, WIDTH, WIDTH), BF16),
         pltpu.VMEM(elem, F32),
@@ -562,25 +542,18 @@
         pltpu.VMEM((10, 8, WIDTH), F32),
         pltpu.VMEM((NZ, 2, WIDTH), F32),
         pltpu.VMEM((NZ, 1, LANES), F32),
-        pltpu.VMEM((NY * NX, 4, 8, LANES), F32),
-        pltpu.VMEM((NY * NX, 4, 8, LANES), F32),
-        pltpu.VMEM((NY * NX, 1, LANES), F32),
+        pltpu.VMEM((NY * NX, 9, 8, LANES), F32),
         pltpu.VMEM((2, 16, WIDTH), F32),
         pltpu.VMEM((2, 16, WIDTH), F32),
         pltpu.VMEM((2, 16, WIDTH), F32),
         dma((22,)),
         dma((2,)),
-        dma((8,)),
         dma((6,)),
         dma((6,)),
         dma((7,)),
         dma((7,)),
         dma((7,)),
         dma((7,)),
-        dma((15,)),
-        dma((15,)),
-        dma((15,)),
-        dma((15,)),
         dma((15,)),
         dma((15,)),
         dma((4,)),
@@ -596,7 +569,7 @@
     ]
     new_disp, new_vel, kernel = pl.pallas_call(
         body,
-        out_shape=[pltpu.VMEM(t.shape, F32) for t in shapes],
+        out_shape=[pltpu.VMEM(shape, F32) for shape in (node, node, elem)],
         in_specs=[pl.BlockSpec(memory_space=pltpu.HBM)] * 10,
         out_specs=[pl.BlockSpec(memory_space=pltpu.VMEM)] * 3,
         scratch_shapes=scratch,
@@ -621,7 +594,7 @@
         out_shape=shapes,
         in_specs=[pl.BlockSpec(memory_space=pltpu.VMEM)] * 3,
         out_specs=[pl.BlockSpec(memory_space=pltpu.HBM)] * 3,
-        scratch_shapes=[dma((3,))],
+        scratch_shapes=[dma((9,))],
         name="results",
     )(*(pltpu.with_memory_space_constraint(x, pltpu.VMEM) for x in (new_disp, new_vel, kernel)))
     return tuple(jnp.transpose(out, (1, 0, 2)) for out in outs)

time: 30.8 us -> 30.6 us (level)
  no operation moved by 1% of the time
where the time goes in v5:
time: 30.6 us; the launch traced here: 30.5 us
  Pallas kernels  29.2 us (95%)
  between operations  1.29 us (4%)
    pallas_call x1, Pallas kernels, per_device(): pl.pallas_call(body, out_shape=[pltpu.VMEM(shape, F32) for shape in (node...  28.2 us
    pallas_call x1, Pallas kernels, per_device(): pl.pallas_call(finish, out_shape=shapes, in_specs=[pl.BlockSpec(memory_sp...  1 us

profile of v5, /device:TPU:1, one launch (start us, length us, event | category | flops | bytes accessed | tf_op | source)
XLA Modules:
  0.0 30.5 jit_solution(13428178912234395818)
XLA Ops:
  1.3 28.2 %adjoint_steps.1 = (f32[4,33,4,128]{3,2,1,0:T(4,128)S(1)}, f32[4,33,4,128]{3,2,1,0:T(4,128)S(1)}, f32[25,8,512]{2,1,0:T(8,128)S(1)}) custom-call(f32[33,4,512]{2,1,0:T(4,128)} %bitcast.9, f32[33,4,512]{2,1,0:T(4,128)} %bitcast.10, f32[2,33,4,512]{3,2,1,0:T(4,128)} %bitcast.7, f32[25,8,512]{2,1,0:T(8,128)} %bitcast.8, f32[8,25]{1,0:T(8,128)} %inv_rad.1, ...), custom_call_target="tpu_custom_call" | custom-call | tf_op jit(solution)/shard_map/adjoint_steps/pallas_call | solution.py:570
  29.5 1.0 %results.1 = (f32[33,4,512]{2,1,0:T(4,128)}, f32[33,4,512]{2,1,0:T(4,128)}, f32[25,8,512]{2,1,0:T(8,128)}) custom-call(f32[4,33,4,128]{3,2,1,0:T(4,128)S(1)} %get-tuple-element.9.a, f32[4,33,4,128]{3,2,1,0:T(4,128)S(1)} %get-tuple-element.10.b, f32[25,8,512]{2,1,0:T(8,128)S(1)} %get-tuple-element.11.c), custom_call_target="tpu_custom_call" | custom-call | tf_op jit(solution)/shard_map/results/pallas_call | solution.py:592
